TPU v7x, 256 devices: a whole 4x4x8 slice. The times are simulated.
256 devices in a mesh: gx: 16 (over z, x_lo), gy: 2 (over core), gz: 8 (over y, x_hi).
Axes of the slice: x: 4 (x_hi: 2, x_lo: 2; x = x_hi * 2 + x_lo), y: 4, z: 8, core: 2. Of those that a mesh axis runs over, the one named last changes fastest.
Arguments:
- field: bfloat16 [32, 384, 96, 1024], P(None, 'gx', 'gy', 'gz'), may hold values from -6 to 6
- start_first: float32 [384, 64], replicated, may hold values from -0.3125 to 0.3125
- factor_second: bfloat16 [96, 64], replicated, may hold values from -0.625 to 0.625
- factor_third: bfloat16 [1024, 64], replicated, may hold values from -0.1875 to 0.1875
- factor_vars: bfloat16 [32, 16], replicated, may hold values from -1 to 1
Outputs:
- first_factor: float32 [384, 64], replicated
- core: float32 [64, 64, 64, 16], P('gx', 'gy', 'gz')
All inputs are finite; a program needn't handle non-finite values.
Results may differ from a plain program's by a relative error of at most 0.0031.
Values sent between devices are 32-bit elements; how exact they have to be, the bound alone decides.
No kernel may reach another device: no remote copies, remote signals or barrier semaphores. Data moves between devices by JAX's collectives and lax.ppermute only.
A program may use at most 192 MiB of HBM per device.

v0:
```python
import jax
import jax.numpy as jnp
from jax import lax
from jax.sharding import PartitionSpec as P

SUB = 3
CX = 24
CY = 48
CZ = 128


highest = lax.Precision.HIGHEST


def orthonormal_steps(gram_matrix, current):
    for repeat in range(SUB):
        product = jnp.dot(
            gram_matrix, current, precision=highest, preferred_element_type=jnp.float32
        )
        inner_gram = jnp.dot(
            product.T, product, precision=highest, preferred_element_type=jnp.float32
        )
        lower_factor = jnp.linalg.cholesky(inner_gram)
        current = jax.scipy.linalg.solve_triangular(lower_factor, product.T, lower=True).T
    return current


def column_gram(block):
    return lax.dot_general(
        block,
        block,
        (((0,), (0,)), ((), ())),
        precision=highest,
        preferred_element_type=jnp.float32,
    )


def per_device(field, start_first, factor_second, factor_third, factor_vars):
    reduced = jnp.einsum(
        "lijk,le->eijk", field, factor_vars, preferred_element_type=jnp.float32
    ).astype(jnp.bfloat16)
    local_third = lax.dynamic_slice_in_dim(factor_third, lax.axis_index("gz") * CZ, CZ, 0)
    local_second = lax.dynamic_slice_in_dim(factor_second, lax.axis_index("gy") * CY, CY, 0).astype(
        jnp.float32
    )
    columns = local_third
    depth = lax.psum_scatter(
        jnp.einsum("eijk,kc->ceij", reduced, columns, preferred_element_type=jnp.float32),
        "gz",
        scatter_dimension=0,
        tiled=True,
    )
    columns = local_second
    projected = lax.psum_scatter(
        jnp.einsum(
            "ceij,jb->bcei", depth, columns, precision=highest, preferred_element_type=jnp.float32
        ),
        "gy",
        scatter_dimension=0,
        tiled=True,
    )
    column_block = projected.reshape(-1, CX)
    gathered = lax.all_gather(column_block, "gx", axis=1, tiled=True)
    gram_matrix = lax.psum(column_gram(gathered), ("gy", "gz"))
    first_factor = orthonormal_steps(gram_matrix, start_first)
    local_first = lax.dynamic_slice_in_dim(first_factor, lax.axis_index("gx") * CX, CX, 0)
    columns = local_first
    core = lax.psum_scatter(
        jnp.einsum(
            "bcei,ia->abce",
            projected,
            columns,
            precision=highest,
            preferred_element_type=jnp.float32,
        ),
        "gx",
        scatter_dimension=0,
        tiled=True,
    )
    return (first_factor, core)


def solution(mesh):
    in_specs = (P(None, "gx", "gy", "gz"), P(), P(), P(), P())
    out_specs = (P(), P("gx", "gy", "gz", None))
    return jax.shard_map(
        per_device, mesh=mesh, in_specs=in_specs, out_specs=out_specs, check_vma=False
    )
```

profile of v0, /device:TPU:2, one launch (start us, length us, event | category | flops | bytes accessed | tf_op | source)
XLA Modules:
  0.0 673.6 jit_solution(6807553839199053047)
XLA Ops:
  7.2 0.0 reduce-scatter.6.cloned.1.call-start
  7.2 9.4 %fusion.4 = bf16[16,24,48,128]{3,0,2,1:T(8,128)(2,1)S(1)} fusion(bf16[32,24,48,128]{3,2,1,0:T(8,128)(2,1)} %param.8, bf16[32,16]{0,1:T(8,128)(2,1)} %param.12), kind=kOutput, calls=%fused_computation.4 | convolution fusion | flops 153354240 | bytes 14156800 | tf_op jit(solution)/shard_map/lijk,le->eijk/dot_general | solution.py:39
  16.6 10.3 %fusion.2 = f32[64,16,24,48]{3,0,2,1:T(8,128)} fusion(bf16[16,24,48,128]{3,0,2,1:T(8,128)(2,1)S(1)} %fusion.4, bf16[1024,64]{0,1:T(8,128)(2,1)S(1)} %copy-done, s32[]{:T(128)S(6)} %select_n.13), kind=kOutput, calls=%fused_computation.2 | convolution fusion | flops 301989888 | bytes 9453572 | tf_op jit(solution)/shard_map/eijk,kc->ceij/dot_general | solution.py:48
  26.9 0.0 reduce-scatter.6.cloned.1.call-update
  26.9 0.0 reduce-scatter.10.cloned.1.call-start
  26.9 158.9 %reduce-scatter.6.cloned.1.call-done = f32[8,16,24,48]{3,0,2,1:T(8,128)} async-done(((f32[64,16,24,48]{3,0,2,1:T(8,128)}), f32[8,16,24,48]{3,0,2,1:T(8,128)}) %reduce-scatter.6.cloned.1.call-update) | async-done | bytes 589840 | tf_op jit(solution)/shard_map/reduce_scatter | solution.py:47
  185.8 2.4 fusion.7
  188.2 1.3 copy.37
  189.6 0.0 reduce-scatter.10.cloned.1.call-update
  189.6 0.2 all-gather.2.cloned.1.call-start
  189.8 12.3 %reduce-scatter.10.cloned.1.call-done = f32[32,3072]{1,0:T(8,128)} async-done(((f32[64,3072]{1,0:T(8,128)}), f32[32,3072]{1,0:T(8,128)}) %reduce-scatter.10.cloned.1.call-update) | async-done | bytes 393232
  202.1 1.5 copy.38
  203.6 2.6 copy.24
  206.2 4.4 reshape.15
  210.6 0.0 all-gather.2.cloned.1.call-update
  210.6 0.0 all-reduce.2.cloned.1.call-start
  210.7 141.4 %all-gather.2.cloned.1.call-done = f32[4096,384]{0,1:T(8,128)} async-done(((f32[4096,24]{0,1:T(8,128)}), f32[4096,384]{0,1:T(8,128)}) %all-gather.2.cloned.1.call-update) | async-done | bytes 6291472 | tf_op jit(solution)/shard_map/all_gather | solution.py:63
  352.1 14.1 %fusion.39 = f32[384,384]{1,0:T(8,128)} fusion(f32[4096,384]{0,1:T(8,128)} %all-gather.2.cloned.1.call-done), kind=kOutput, calls=%fused_computation.49 | convolution fusion | flops 7247757312 | bytes 6881280 | tf_op jit(solution)/shard_map/dot_general | solution.py:29
  366.2 0.3 reduce-scatter.8.cloned.1.call-start
  366.5 150.6 %all-reduce.2.cloned.1.call-done = f32[384,384]{1,0:T(8,128)} async-done(((f32[384,384]{1,0:T(8,128)}), f32[384,384]{1,0:T(8,128)}) %all-reduce.2.cloned.1.call-update) | async-done | bytes 589840 | tf_op jit(solution)/shard_map/psum | solution.py:64
  517.1 1.8 fusion.40
  518.9 0.2 fusion.41
  519.1 0.1 copy.25
  519.2 5.8 cholesky.59
  525.1 0.6 compare_reduce_fusion.2
  525.7 0.7 fusion.15
  526.4 4.9 custom-call.7
  531.3 0.3 fusion.13
  531.6 1.8 fusion.42
  533.4 0.2 fusion.43
  533.7 0.1 copy.26
  533.8 5.8 cholesky.70
  539.6 0.6 compare_reduce_fusion.1
  540.3 0.7 fusion.16
  541.0 4.9 custom-call.8
  545.9 0.3 fusion.11
  546.2 1.8 fusion.44
  548.0 0.2 fusion.45
  548.2 0.1 copy.27
  548.3 5.8 cholesky.81
  554.2 0.6 compare_reduce_fusion
  554.8 0.7 fusion.17
  555.5 4.9 custom-call.9
  560.4 0.3 fusion.9
  560.7 3.5 fusion.18
  564.2 4.4 copy.29
  568.6 0.0 reduce-scatter.8.cloned.1.call-update
  568.6 98.5 %reduce-scatter.8.cloned.1.call-done = f32[4,32,8,16]{1,3,2,0:T(8,128)} async-done(((f32[64,32,8,16]{1,3,2,0:T(8,128)}), f32[4,32,8,16]{1,3,2,0:T(8,128)}) %reduce-scatter.8.cloned.1.call-update) | async-done | bytes 65552 | tf_op jit(solution)/shard_map/reduce_scatter | solution.py:68
  (15 shorter events, 0.2 us)
Async XLA Ops:
  7.2 9.4 %copy-start = (bf16[1024,64]{0,1:T(8,128)(2,1)S(1)}, bf16[1024,64]{0,1:T(8,128)(2,1)}, u32[]{:S(2)}) copy-start(bf16[1024,64]{0,1:T(8,128)(2,1)} %param.11) | copy-start | bytes 393220
  7.2 178.6 %reduce-scatter.6.cloned.1.call-start = ((), (), s32[]{:S(2)}) async-start(), calls=%async_computation.3 | async-start | bytes 14155776 | tf_op jit(solution)/shard_map/reduce_scatter | solution.py:47
  26.9 158.9 %copy-start.3 = (bf16[96,64]{0,1:T(8,128)(2,1)S(1)}, bf16[96,64]{0,1:T(8,128)(2,1)}, u32[]{:S(2)}) copy-start(bf16[96,64]{0,1:T(8,128)(2,1)} %param.10) | copy-start | bytes 36868
  26.9 175.3 %reduce-scatter.10.cloned.1.call-start = ((), (), s32[]{:S(2)}) async-start(), calls=%async_computation.7 | async-start | bytes 1179648
  189.6 162.5 %all-gather.2.cloned.1.call-start = ((), (), s32[]{:S(2)}) async-start(), calls=%async_computation.4 | async-start | bytes 6684672 | tf_op jit(solution)/shard_map/all_gather | solution.py:63
  210.6 306.4 %copy-start.2 = (f32[384,64]{0,1:T(8,128)S(1)}, f32[384,64]{0,1:T(8,128)}, u32[]{:S(2)}) copy-start(f32[384,64]{0,1:T(8,128)} %param.9) | copy-start | bytes 294916
  210.6 306.4 %all-reduce.2.cloned.1.call-start = ((), (), s32[]{:S(2)}) async-start(), calls=%async_computation.5 | async-start | bytes 1179648 | tf_op jit(solution)/shard_map/psum | solution.py:64
  366.2 300.9 %reduce-scatter.8.cloned.1.call-start = ((), (), s32[]{:S(2)}) async-start(), calls=%async_computation.6 | async-start | bytes 4456448 | tf_op jit(solution)/shard_map/reduce_scatter | solution.py:68
  560.7 7.9 %copy-start.1 = (f32[64,384]{1,0:T(8,128)}, f32[64,384]{1,0:T(8,128)S(1)}, u32[]{:S(2)}) copy-start(f32[64,384]{1,0:T(8,128)S(1)} %fusion.9) | copy-start | bytes 294916
Sparse Core Ops, SparseCore 0:
  27.0 158.7 reduce-scatter.5
  189.7 12.4 reduce-scatter.9
  210.7 141.2 all-gather.1
  366.3 150.7 all-reduce.1
  568.7 98.3 reduce-scatter.7
where the time goes:
time: 676 us; the launch traced here: 674 us
  waiting for transfers between devices  562 us (83%)
  matrix products  46.7 us (7%)
  other arithmetic  36.2 us (5%)
  local copies, waits for them, and re-layouts  14.4 us (2%)
  between operations  14 us (2%)
    reduce_scatter x1, waiting for transfers between devices, per_device(): lax.psum_scatter(jnp.einsum('eijk,kc->ceij', reduced, columns, preferred_...  159 us
    psum x1, waiting for transfers between devices, per_device(): gram_matrix = lax.psum(column_gram(gathered), ('gy', 'gz'))  151 us
    all_gather x1, waiting for transfers between devices, per_device(): gathered = lax.all_gather(column_block, 'gx', axis=1, tiled=True)  141 us
    reduce_scatter x1, waiting for transfers between devices, per_device(): lax.psum_scatter(jnp.einsum('bcei,ia->abce', projected, columns, precisio...  98.5 us
    another operation x9, other arithmetic, orthonormal_steps(): lower_factor = jnp.linalg.cholesky(inner_gram)  19.6 us
    another operation x6, other arithmetic, orthonormal_steps(): jax.scipy.linalg.solve_triangular(lower_factor, product.T, lower=True)  16.6 us
    dot_general x1, matrix products, column_gram(): lax.dot_general(block, block, (((0,), (0,)), ((), ())), precision=highest...  14.1 us
  transfers between devices with their start and end apart: 5, of which 5 were waited for; matrix products, arithmetic and copies ran while one was open for 0% of the time, Pallas kernels for 0%

commit v1 on v0

v1 whole, which is shorter than its diff:
```python
import functools

import jax
import jax.numpy as jnp
from jax import lax
from jax.experimental import pallas as pl
from jax.experimental.pallas import tpu as pltpu
from jax.sharding import PartitionSpec as P

SUB = 3
R = 64
RV = 16
V = 32
CX = 24
CY = 48
CZ = 128
GX = 16
GZ = 8
HALF = CX // 2
EH = RV // 2
NX = 384
IB = 4
IPB = 2
BLOCKS = ((0, 0), (0, 1), (0, 2), (1, 1), (1, 2), (2, 2))

f32 = jnp.float32
bf16 = jnp.bfloat16
highest = lax.Precision.HIGHEST


def iota(shape, dim):
    return lax.broadcasted_iota(jnp.int32, shape, dim)


def onehot(condition):
    return jnp.where(condition, 1.0, 0.0).astype(bf16)


def dot(a, b, contract=(1, 0), precision=None):
    return lax.dot_general(
        a, b, (((contract[0],), (contract[1],)), ((), ())), precision=precision, preferred_element_type=f32
    )


def depth_kernel(field_ref, third_ref, vars_ref, keep_ref, send_ref, mix_ref, cols_ref, left_ref):
    gy = lax.axis_index("gy")
    gz = lax.axis_index("gz")

    @pl.when(pl.program_id(0) == 0)
    def _():
        rows = iota((256, RV), 0)
        pick_e = onehot(((rows >> 4) + EH * gy) & (RV - 1) == iota((256, RV), 1))
        wide = dot(pick_e, vars_ref[...], (1, 1)).astype(bf16)
        spread = onehot(iota((V, 512), 0) == iota((V, 512), 1) >> 4)
        full = dot(wide, spread)
        same_j = (iota((256, 512), 0) & 15) == (iota((256, 512), 1) & 15)
        mix_ref[...] = jnp.where(same_j, full, 0.0).astype(bf16)
        third = third_ref[pl.ds(pl.multiple_of(gz * CZ, CZ), CZ), :]
        spread = onehot(iota((R, 512), 0) == iota((R, 512), 1) >> 3)
        full = dot(third, spread)
        which = iota((CZ, 512), 1) & 7
        for e in range(EH):
            cols_ref[e * CZ : (e + 1) * CZ, :] = jnp.where(which == e, full, 0.0).astype(bf16)

    mix = mix_ref[...]
    for pair in range(IB // 2):
        for jb in range(CY // 16):
            pieces = [
                field_ref[:, 2 * pair + s, jb * 16 : jb * 16 + 16, :].reshape(512, CZ) for s in range(2)
            ]
            reduced = dot(mix, jnp.concatenate(pieces, axis=1)).astype(bf16)
            for h in range(2):
                for s in range(2):
                    top = (h * IB + 2 * pair + s) * CY + jb * 16
                    for e in range(EH):
                        left_ref[top : top + 16, e * CZ : (e + 1) * CZ] = reduced[
                            (h * EH + e) * 16 : (h * EH + e + 1) * 16, s * CZ : (s + 1) * CZ
                        ]
    depth = dot(left_ref[...], cols_ref[...])
    keep_ref[...] = depth[: IB * CY].reshape(IB, CY, 512)
    send_ref[...] = depth[IB * CY :].reshape(IB, CY, 512)


def local_depth(field, factor_third, factor_vars):
    half = jax.ShapeDtypeStruct((CX, CY, 512), f32)
    block = pl.BlockSpec((IB, CY, 512), lambda i: (i, 0, 0))
    return pl.pallas_call(
        depth_kernel,
        grid=(CX // IB,),
        in_specs=[
            pl.BlockSpec((V, IB, CY, CZ), lambda i: (0, i, 0, 0)),
            pl.BlockSpec((1024, R), lambda i: (0, 0)),
            pl.BlockSpec((V, RV), lambda i: (0, 0)),
        ],
        out_specs=[block, block],
        out_shape=[half, half],
        scratch_shapes=[
            pltpu.VMEM((256, 512), bf16),
            pltpu.VMEM((1024, 512), bf16),
            pltpu.VMEM((2 * IB * CY, 1024), bf16),
        ],
        compiler_params=pltpu.CompilerParams(vmem_limit_bytes=48 * 2**20),
        cost_estimate=pl.CostEstimate(flops=8 * 10**9, bytes_accessed=14 * 2**20, transcendentals=0),
        name="depth",
    )(field, factor_third, factor_vars)


def split(x):
    high = x.astype(bf16)
    return high, (x - high.astype(f32)).astype(bf16)


def project_kernel(keep_ref, recv_ref, second_ref, out_ref, weights_ref):
    gy = lax.axis_index("gy")

    @pl.when(pl.program_id(0) == 0)
    def _():
        rows = iota((R, R), 0)
        rank = ((rows >> 1) & 1) * 32 + (rows >> 2) * 2 + (rows & 1)
        pick = onehot(rank == iota((R, R), 1))
        own = second_ref[pl.ds(pl.multiple_of(gy * CY, 16), CY), :]
        other = second_ref[pl.ds(pl.multiple_of((1 - gy) * CY, 16), CY), :]
        stacked = jnp.concatenate([own, other, own, other], axis=0)
        weights_ref[...] = dot(pick, stacked, (1, 1)).astype(bf16)

    weights = weights_ref[...]
    low_lanes = iota((R, 128), 1) < 64
    for ip in range(IPB):
        sides = []
        for s in range(2):
            keep_high, keep_low = split(keep_ref[s, ip])
            recv_high, recv_low = split(recv_ref[s, ip])
            sides.append(dot(weights, jnp.concatenate([keep_high, recv_high, keep_low, recv_low], axis=0)))
        for q in range(4):
            first = sides[0][:, q * 128 : (q + 1) * 128]
            second = sides[1][:, q * 128 : (q + 1) * 128]
            even = jnp.where(low_lanes, first, pltpu.roll(second, 64, 1))
            odd = jnp.where(low_lanes, pltpu.roll(first, 64, 1), second)
            for g in range(GX):
                out_ref[2 * q, g, ip * 4 : ip * 4 + 4, :] = even[4 * g : 4 * g + 4, :]
                out_ref[2 * q + 1, g, ip * 4 : ip * 4 + 4, :] = odd[4 * g : 4 * g + 4, :]


def local_projected(keep, recv, factor_second):
    block = pl.BlockSpec((2, IPB, CY, 512), lambda i: (0, i, 0, 0))
    return pl.pallas_call(
        project_kernel,
        grid=(HALF // IPB,),
        in_specs=[block, block, pl.BlockSpec((2 * CY, R), lambda i: (0, 0))],
        out_specs=pl.BlockSpec((GZ, GX, 4 * IPB, 128), lambda i: (0, 0, i, 0)),
        out_shape=jax.ShapeDtypeStruct((GZ, GX, 4 * HALF, 128), f32),
        scratch_shapes=[pltpu.VMEM((R, 4 * CY), bf16)],
        compiler_params=pltpu.CompilerParams(vmem_limit_bytes=48 * 2**20),
        cost_estimate=pl.CostEstimate(flops=10**9, bytes_accessed=8 * 2**20, transcendentals=0),
        name="projected",
    )(keep.reshape(2, HALF, CY, 512), recv.reshape(2, HALF, CY, 512), factor_second)


def gram_kernel(rows_ref, gram_ref, keep_ref, send_ref, columns_ref):
    gy = lax.axis_index("gy")
    low_lanes = iota((GX * HALF, 128), 1) < 64
    for t in range(2):
        first = rows_ref[pl.ds(2 * t, GX * HALF, stride=4), :]
        second = rows_ref[pl.ds(2 * t + 1, GX * HALF, stride=4), :]
        sides = (
            jnp.where(low_lanes, first, pltpu.roll(second, 64, 1)),
            jnp.where(low_lanes, pltpu.roll(first, 64, 1), second),
        )
        for s in range(2):
            for g in range(GX):
                top = g * CX + s * HALF
                columns_ref[top : top + HALF, t * 128 : (t + 1) * 128] = sides[s][g * HALF : (g + 1) * HALF, :]
    for n, (r, c) in enumerate(BLOCKS):
        gram_ref[n * 128 : (n + 1) * 128, :] = dot(
            columns_ref[r * 128 : (r + 1) * 128, :], columns_ref[c * 128 : (c + 1) * 128, :], (1, 1), highest
        )
    low, high = columns_ref[:, :128], columns_ref[:, 128:]
    keep_ref[...] = jnp.where(gy == 0, low, high)
    send_ref[...] = jnp.where(gy == 0, high, low)


def local_gram(rows):
    half = jax.ShapeDtypeStruct((NX, 128), f32)
    return pl.pallas_call(
        gram_kernel,
        out_shape=[jax.ShapeDtypeStruct((768, 128), f32), half, half],
        scratch_shapes=[pltpu.VMEM((NX, 256), f32)],
        name="gram",
    )(rows)


def invert_lower(matrix):
    row = iota((R, 128), 0)
    lane = iota((R, 128), 1)
    work = jnp.concatenate([matrix, jnp.where(iota((R, R), 0) == iota((R, R), 1), 1.0, 0.0)], axis=1)
    pivots = jnp.ones((R, 1), f32)
    for j in range(R):
        pivot_row = work[j : j + 1, :]
        pivot = work[j : j + 1, j : j + 1]
        factor = jnp.where(row[:, :1] > j, work[:, j : j + 1] / pivot, 0.0)
        pivots = jnp.where(row[:, :1] == j, pivot, pivots)
        work = work - factor * pivot_row
    return work[:, R:] * lax.rsqrt(pivots)


def factor_kernel(gram_ref, start_ref, keep_ref, recv_ref, factor_ref, core_ref, full_ref):
    gy = lax.axis_index("gy")
    for n, (r, c) in enumerate(BLOCKS):
        block = gram_ref[n * 128 : (n + 1) * 128, :]
        full_ref[r * 128 : (r + 1) * 128, c * 128 : (c + 1) * 128] = block
        if r != c:
            full_ref[c * 128 : (c + 1) * 128, r * 128 : (r + 1) * 128] = block.T
    basis = start_ref[...]
    for _ in range(SUB):
        product = dot(full_ref[...], basis, precision=highest)
        inner = dot(product, product, (0, 0), highest)
        basis = dot(product, invert_lower(inner), (1, 1), highest)
    factor_ref[...] = basis
    keep, recv = keep_ref[...], recv_ref[...]
    columns = jnp.concatenate([jnp.where(gy == 0, keep, recv), jnp.where(gy == 0, recv, keep)], axis=1)
    core_ref[...] = dot(basis, columns, (0, 0), highest)


def factor_and_core(gram, start, keep, recv):
    return pl.pallas_call(
        factor_kernel,
        out_shape=[jax.ShapeDtypeStruct((NX, R), f32), jax.ShapeDtypeStruct((R, 256), f32)],
        scratch_shapes=[pltpu.VMEM((NX, NX), f32)],
        name="factor",
    )(gram, start, keep, recv)


def swap(x):
    return lax.ppermute(x, "gy", [(0, 1), (1, 0)])


def exchange(x, axes):
    return lax.all_to_all(x, axes, 0, 0, tiled=True)


def per_device(field, start_first, factor_second, factor_third, factor_vars):
    keep, send = local_depth(field, factor_third, factor_vars)
    partial = local_projected(keep, swap(send), factor_second)
    projected = jnp.sum(exchange(partial, "gz"), axis=0)
    rows = exchange(projected, "gx").reshape(GX * HALF * 4, 128)
    gram, keep, send = local_gram(rows)
    recv = swap(send)
    gram = jnp.sum(exchange(gram.reshape(16, 48, 128), ("gy", "gz")), axis=0)
    gram = jnp.sum(exchange(jnp.broadcast_to(gram, (16, 48, 128)), "gx"), axis=0)
    gram = exchange(jnp.broadcast_to(gram, (16, 48, 128)), ("gy", "gz")).reshape(768, 128)
    first_factor, core = factor_and_core(gram, start_first, keep, recv)
    core = exchange(core.reshape(GX, 4, 256), "gx")
    core = core.reshape(GX, 4, 2, 2, 8, EH).transpose(1, 0, 3, 4, 2, 5)
    return first_factor, core.reshape(4, 32, 8, RV)


def solution(mesh):
    in_specs = (P(None, "gx", "gy", "gz"), P(), P(), P(), P())
    out_specs = (P(), P("gx", "gy", "gz", None))
    return jax.shard_map(per_device, mesh=mesh, in_specs=in_specs, out_specs=out_specs, check_vma=False)
```

time: 676 us -> 185 us (0.27)
  waiting for transfers between devices: 562 us -> 20 us
  blocking collectives: 0 us -> 99.8 us
  matrix products: 46.7 us -> 0 us
  Pallas kernels: 0 us -> 43.5 us
  other arithmetic: 36.2 us -> 0.25 us
  between operations: 14 us -> 0.72 us
  starting transfers between devices: 0.61 us -> 9.47 us
    reduce_scatter x2 -> x0, waiting for transfers between devices: 257 us -> none  [the longest x1 159 us: per_device(): lax.psum_scatter(jnp.einsum('eijk,kc->ceij', reduced, columns, preferred_...]
    psum x1 -> x0, waiting for transfers between devices: 151 us -> none  [per_device(): gram_matrix = lax.psum(column_gram(gathered), ('gy', 'gz'))]
    all_gather x1 -> x0, waiting for transfers between devices: 141 us -> none  [per_device(): gathered = lax.all_gather(column_block, 'gx', axis=1, tiled=True)]
    all_to_all x0 -> x4, blocking collectives: none -> 99.8 us  [exchange(): return lax.all_to_all(x, axes, 0, 0, tiled=True)]
    dot_general x11 -> x0, matrix products: 45.8 us -> none  [the longest x1 14.1 us: column_gram(): lax.dot_general(block, block, (((0,), (0,)), ((), ())), precision=highest...]
    pallas_call x0 -> x4, Pallas kernels: none -> 43.5 us  [the longest x1 24.4 us: factor_and_core(): pl.pallas_call(factor_kernel, out_shape=[jax.ShapeDtypeStruct((NX, R), f3...]
    another operation x15 -> x0, other arithmetic: 36.2 us -> none  [the longest x9 19.6 us: orthonormal_steps(): lower_factor = jnp.linalg.cholesky(inner_gram)]
    all_to_all x0 -> x2, waiting for transfers between devices: none -> 15 us  [exchange(): return lax.all_to_all(x, axes, 0, 0, tiled=True)]
  transfers between devices with their start and end apart: 5 -> 4, of which waited for: 5 -> 4; matrix products, arithmetic and copies ran while one was open for 0% -> 1% of each run, Pallas kernels for 0% -> 0%
where the time goes in v1:
time: 185 us; the launch traced here: 184 us
  blocking collectives  99.8 us (54%)
  Pallas kernels  43.5 us (24%)
  waiting for transfers between devices  20 us (11%)
  local copies, waits for them, and re-layouts  10.7 us (6%)
  starting transfers between devices  9.47 us (5%)
    all_to_all x4, blocking collectives, exchange(): return lax.all_to_all(x, axes, 0, 0, tiled=True)  99.8 us
    pallas_call x1, Pallas kernels, factor_and_core(): pl.pallas_call(factor_kernel, out_shape=[jax.ShapeDtypeStruct((NX, R), f3...  24.4 us
    all_to_all x2, waiting for transfers between devices, exchange(): return lax.all_to_all(x, axes, 0, 0, tiled=True)  15 us
    pallas_call x1, Pallas kernels, local_depth(): pl.pallas_call(depth_kernel, grid=(CX // IB,), in_specs=[pl.BlockSpec((V,...  10.2 us
    all_to_all x2, starting transfers between devices, exchange(): return lax.all_to_all(x, axes, 0, 0, tiled=True)  8.79 us
    pallas_call x1, Pallas kernels, local_projected(): pl.pallas_call(project_kernel, grid=(HALF // IPB,), in_specs=[block, bloc...  6.28 us
    unnamed x16, local copies, waits for them, and re-layouts  6.11 us
    ppermute x2, waiting for transfers between devices, swap(): return lax.ppermute(x, 'gy', [(0, 1), (1, 0)])  5.02 us
  transfers between devices with their start and end apart: 4, of which 4 were waited for; matrix products, arithmetic and copies ran while one was open for 1% of the time, Pallas kernels for 0%

profile of v1, /device:TPU:2, one launch (start us, length us, event | category | flops | bytes accessed | tf_op | source)
XLA Modules:
  0.0 184.5 jit_solution(17063112929097095173)
XLA Ops:
  0.6 1.1 copy.29.third_ref
  1.7 0.8 copy.30.vars_ref
  2.5 0.0 copy-start.3
  2.5 10.2 %depth.1 = (f32[24,48,512]{2,1,0:T(8,128)S(1)}, f32[24,48,512]{2,1,0:T(8,128)}) custom-call(bf16[32,24,48,128]{3,2,1,0:T(8,128)(2,1)} %field_ref.1, bf16[1024,64]{1,0:T(8,128)(2,1)S(1)} %copy.29.third_ref, bf16[32,16]{1,0:T(8,128)(2,1)S(1)} %copy.30.vars_ref), custom_call_target="tpu_custom_call" | custom-call | flops 8000000000 | bytes 14680064 | tf_op jit(solution)/shard_map/depth/pallas_call | solution.py:87
  12.7 0.0 collective-permute-start
  12.7 0.0 copy-done.3
  12.7 0.1 copy.31.second_ref
  12.8 4.8 %collective-permute-done = f32[24,48,512]{2,1,0:T(8,128)} collective-permute-done((f32[24,48,512]{2,1,0:T(8,128)}, f32[24,48,512]{2,1,0:T(8,128)}, u32[]{:S(2)}, u32[]{:S(2)}) %collective-permute-start) | collective-permute-done | bytes 2359328 | tf_op jit(solution)/shard_map/ppermute | solution.py:234
  17.5 6.3 %projected.1 = f32[8,16,48,128]{3,2,1,0:T(8,128)} custom-call(f32[2,12,48,512]{3,2,1,0:T(8,128)S(1)} %bitcast.8, f32[2,12,48,512]{3,2,1,0:T(8,128)} %bitcast.1.recv_ref, bf16[96,64]{1,0:T(8,128)(2,1)S(1)} %copy.31.second_ref), custom_call_target="tpu_custom_call" | custom-call | flops 1000000000 | bytes 8388608 | tf_op jit(solution)/shard_map/projected/pallas_call | solution.py:146
  23.8 46.0 %all_to_all.30 = f32[8,16,48,128]{3,2,1,0:T(8,128)S(1)} all-to-all(f32[8,16,48,128]{3,2,1,0:T(8,128)} %projected.1), channel_id=1, replica_groups=mesh['gx'=16,'gy'=2,'gz'=8] {'gz'}, dimensions={0} | all-to-all | bytes 6291456 | tf_op jit(solution)/shard_map/all_to_all | solution.py:238
  69.8 0.2 reduce_sum.27
  70.0 0.0 copy-start.2
  70.0 22.1 %all_to_all.31 = f32[16,48,128]{2,1,0:T(8,128)} all-to-all(f32[16,48,128]{2,1,0:T(8,128)S(1)} %reduce_sum.27), channel_id=1, replica_groups=mesh['gx'=16,'gy'=2,'gz'=8] {'gx'}, dimensions={0} | all-to-all | bytes 786432 | tf_op jit(solution)/shard_map/all_to_all | solution.py:238
  92.2 2.7 %gram.1 = (f32[768,128]{1,0:T(8,128)}, f32[384,128]{1,0:T(8,128)}, f32[384,128]{1,0:T(8,128)}) custom-call(f32[768,128]{1,0:T(8,128)} %bitcast.10), custom_call_target="tpu_custom_call" | custom-call | tf_op jit(solution)/shard_map/gram/pallas_call | solution.py:184
  94.9 0.0 copy-start.4
  94.9 14.2 %all_to_all.32 = f32[16,48,128]{2,1,0:T(8,128)S(1)} all-to-all(f32[16,48,128]{2,1,0:T(8,128)} %bitcast.12), channel_id=1, replica_groups=mesh['gx'=16,'gy'=2,'gz'=8] {'gy','gz'}, dimensions={0} | all-to-all | bytes 786432 | tf_op jit(solution)/shard_map/all_to_all | solution.py:238
  109.2 17.4 %all_to_all.33 = f32[16,48,128]{2,1,0:T(8,128)S(1)} all-to-all(f32[16,48,128]{2,1,0:T(8,128)S(1)} %broadcast_in_dim.6), channel_id=1, replica_groups=mesh['gx'=16,'gy'=2,'gz'=8] {'gx'}, dimensions={0} | all-to-all | bytes 786432 | tf_op jit(solution)/shard_map/all_to_all | solution.py:238
  126.7 0.8 broadcast_in_dim.7
  127.4 3.7 %all-to-all-start.4 = ((f32[16,48,128]{2,1,0:T(8,128)}), f32[16,48,128]{2,1,0:T(8,128)S(1)}, u32[]{:S(2)}, u32[]{:S(2)}) async-start(f32[16,48,128]{2,1,0:T(8,128)} %broadcast_in_dim.7), calls=%async_computation.4 | async-start | bytes 786432 | tf_op jit(solution)/shard_map/all_to_all | solution.py:238
  131.1 0.0 copy-done.4
  131.2 0.7 collective-permute-start.1
  131.8 0.0 copy-done.2
  131.8 0.8 copy.32.start_ref
  132.6 0.3 collective-permute-done.1.recv_ref
  132.9 0.0 copy-start.1
  132.9 8.9 %all-to-all-done.4 = f32[16,48,128]{2,1,0:T(8,128)S(1)} async-done(((f32[16,48,128]{2,1,0:T(8,128)}), f32[16,48,128]{2,1,0:T(8,128)S(1)}, u32[]{:S(2)}, u32[]{:S(2)}) %all-to-all-start.4) | async-done | bytes 393248 | tf_op jit(solution)/shard_map/all_to_all | solution.py:238
  141.8 0.0 copy-start
  141.8 0.0 copy-done.1
  141.8 0.7 copy-done
  142.6 24.4 %factor.1 = (f32[384,64]{1,0:T(8,128)}, f32[64,256]{1,0:T(8,128)}) custom-call(f32[768,128]{1,0:T(8,128)} %bitcast.11, f32[384,64]{1,0:T(8,128)} %copy.32.start_ref, f32[384,128]{1,0:T(8,128)} %get-tuple-element.12.keep_ref, f32[384,128]{1,0:T(8,128)} %copy-done.1), custom_call_target="tpu_custom_call" | custom-call | tf_op jit(solution)/shard_map/factor/pallas_call | solution.py:225
  166.9 1.5 reshape.33
  168.4 5.1 %all-to-all-start.5 = ((f32[16,4,256]{2,1,0:T(4,128)}), f32[16,4,256]{2,1,0:T(4,128)S(1)}, u32[]{:S(2)}, u32[]{:S(2)}) async-start(f32[16,4,256]{2,1,0:T(4,128)} %reshape.33), calls=%async_computation.5 | async-start | bytes 131072 | tf_op jit(solution)/shard_map/all_to_all | solution.py:238
  173.5 1.7 copy.35
  175.2 6.1 %all-to-all-done.5 = f32[16,4,256]{2,1,0:T(4,128)S(1)} async-done(((f32[16,4,256]{2,1,0:T(4,128)}), f32[16,4,256]{2,1,0:T(4,128)S(1)}, u32[]{:S(2)}, u32[]{:S(2)}) %all-to-all-start.5) | async-done | bytes 65568 | tf_op jit(solution)/shard_map/all_to_all | solution.py:238
  181.3 0.2 copy.33
  181.5 1.5 copy.34
  183.0 0.6 reshape.35
  183.6 0.9 copy.36
  (3 shorter events, 0.1 us)
Async XLA Ops:
  2.5 10.2 %copy-start.3 = (bf16[96,64]{0,1:T(8,128)(2,1)S(1)}, bf16[96,64]{0,1:T(8,128)(2,1)}, u32[]{:S(2)}) copy-start(bf16[96,64]{0,1:T(8,128)(2,1)} %param.7) | copy-start | bytes 36868
  12.7 4.9 %collective-permute-start = (f32[24,48,512]{2,1,0:T(8,128)}, f32[24,48,512]{2,1,0:T(8,128)}, u32[]{:S(2)}, u32[]{:S(2)}) collective-permute-start(f32[24,48,512]{2,1,0:T(8,128)} %get-tuple-element.10), channel_id=1, source_target_pairs={{0,8},{8,0},{1,9},{9,1},{2,10},{10,2},{3,11},{11,3},{4,12},{12,4},... | collective-permute-start | bytes 7077896 | tf_op jit(solution)/shard_map/ppermute | solution.py:234
  70.0 61.8 %copy-start.2 = (f32[384,64]{0,1:T(8,128)S(1)}, f32[384,64]{0,1:T(8,128)}, u32[]{:S(2)}) copy-start(f32[384,64]{0,1:T(8,128)} %param.6) | copy-start | bytes 294916
  94.9 36.3 %copy-start.4 = (f32[384,128]{1,0:T(8,128)S(1)}, f32[384,128]{1,0:T(8,128)}, u32[]{:S(2)}) copy-start(f32[384,128]{1,0:T(8,128)} %get-tuple-element.13) | copy-start | bytes 589828
  127.4 14.4 %all-to-all-start.4 = ((f32[16,48,128]{2,1,0:T(8,128)}), f32[16,48,128]{2,1,0:T(8,128)S(1)}, u32[]{:S(2)}, u32[]{:S(2)}) async-start(f32[16,48,128]{2,1,0:T(8,128)} %broadcast_in_dim.7), calls=%async_computation.4 | async-start | bytes 786432 | tf_op jit(solution)/shard_map/all_to_all | solution.py:238
  131.2 1.7 collective-permute-start.1
  132.9 8.9 %copy-start.1 = (f32[384,128]{1,0:T(8,128)}, f32[384,128]{1,0:T(8,128)S(1)}, u32[]{:S(2)}) copy-start(f32[384,128]{1,0:T(8,128)S(1)} %collective-permute-done.1.recv_ref) | copy-start | bytes 589828
  141.8 0.7 copy-start
  168.4 12.9 %all-to-all-start.5 = ((f32[16,4,256]{2,1,0:T(4,128)}), f32[16,4,256]{2,1,0:T(4,128)S(1)}, u32[]{:S(2)}, u32[]{:S(2)}) async-start(f32[16,4,256]{2,1,0:T(4,128)} %reshape.33), calls=%async_computation.5 | async-start | bytes 131072 | tf_op jit(solution)/shard_map/all_to_all | solution.py:238

commit v2 on v1

v2 whole, which is shorter than its diff:
```python
import jax
import jax.numpy as jnp
from jax import lax
from jax.experimental import pallas as pl
from jax.experimental.pallas import tpu as pltpu
from jax.sharding import PartitionSpec as P

SUB = 3
R = 64
RV = 16
V = 32
CX = 24
CY = 48
CZ = 128
GX = 16
GZ = 8
HALF = CX // 2
EH = RV // 2
NX = 384
IPB = 2
STEP = 4
CHUNKS = (4, 8)
BLOCKS = ((0, 0), (0, 1), (0, 2), (1, 1), (1, 2), (2, 2))

f32 = jnp.float32
bf16 = jnp.bfloat16
highest = lax.Precision.HIGHEST


def iota(shape, dim):
    return lax.broadcasted_iota(jnp.int32, shape, dim)


def onehot(condition):
    return jnp.where(condition, 1.0, 0.0).astype(bf16)


def dot(a, b, contract=(1, 0), precision=None):
    return lax.dot_general(
        a, b, (((contract[0],), (contract[1],)), ((), ())), precision=precision, preferred_element_type=f32
    )


def depth_kernel(field_ref, third_ref, vars_ref, keep_ref, send_ref, mix_ref, cols_ref, left_ref):
    gy = lax.axis_index("gy")
    gz = lax.axis_index("gz")

    @pl.when(pl.program_id(0) == 0)
    def _():
        rows = iota((256, RV), 0)
        pick_e = onehot((((rows >> 4) + EH * gy) & (RV - 1)) == iota((256, RV), 1))
        wide = dot(pick_e, vars_ref[...]).astype(bf16)
        spread = onehot(iota((V, 512), 0) == iota((V, 512), 1) >> 4)
        same_j = (iota((256, 512), 0) & 15) == (iota((256, 512), 1) & 15)
        mix_ref[...] = jnp.where(same_j, dot(wide, spread), 0.0).astype(bf16)
        third = third_ref[:, pl.ds(pl.multiple_of(gz * CZ, CZ), CZ)]
        lane = iota((R, 256), 1)
        spread = onehot(iota((R, 256), 0) == (lane >> 5) * 8 + (lane & 7))
        full = dot(third, spread, (0, 0))
        which = (iota((CZ, 256), 1) >> 3) & 3
        for e in range(4):
            cols_ref[e * CZ : (e + 1) * CZ, :] = jnp.where(which == e, full, 0.0).astype(bf16)

    mix = mix_ref[...]
    for ip in range(IPB):
        for jb in range(CY // 16):
            pieces = [field_ref[:, s, ip, jb * 16 : jb * 16 + 16, :].reshape(512, CZ) for s in range(2)]
            reduced = dot(mix, jnp.concatenate(pieces, axis=1)).astype(bf16)
            for e in range(RV):
                for s in range(2):
                    top = ((e // 4 * 2 + s) * IPB + ip) * CY + jb * 16
                    left_ref[top : top + 16, e % 4 * CZ : (e % 4 + 1) * CZ] = reduced[
                        e * 16 : e * 16 + 16, s * CZ : (s + 1) * CZ
                    ]
    cols = cols_ref[...]
    size = 2 * IPB * CY
    for n in range(4):
        depth = dot(left_ref[n * size : (n + 1) * size, :], cols).reshape(2, IPB, CY, 256)
        (keep_ref, send_ref)[n // 2][:, :, :, n % 2 * 256 : (n % 2 + 1) * 256] = depth


def local_depth(field, third, weights, first, count):
    half = jax.ShapeDtypeStruct((2, count, CY, 512), f32)
    block = pl.BlockSpec((2, IPB, CY, 512), lambda i: (0, i, 0, 0))
    return pl.pallas_call(
        depth_kernel,
        grid=(count // IPB,),
        in_specs=[
            pl.BlockSpec((V, 2, IPB, CY, CZ), lambda i: (0, 0, i + first // IPB, 0, 0)),
            pl.BlockSpec((R, 1024), lambda i: (0, 0)),
            pl.BlockSpec((RV, V), lambda i: (0, 0)),
        ],
        out_specs=[block, block],
        out_shape=[half, half],
        scratch_shapes=[
            pltpu.VMEM((256, 512), bf16),
            pltpu.VMEM((512, 256), bf16),
            pltpu.VMEM((8 * IPB * CY, 512), bf16),
        ],
        compiler_params=pltpu.CompilerParams(vmem_limit_bytes=40 * 2**20),
        cost_estimate=pl.CostEstimate(flops=count * 6 * 10**8, bytes_accessed=count * 1200000, transcendentals=0),
        name="depth",
    )(field, third, weights)


def split(x):
    high = x.astype(bf16)
    return high, (x - high.astype(f32)).astype(bf16)


def project_kernel(keep_ref, recv_ref, second_ref, out_ref, weights_ref):
    gy = lax.axis_index("gy")

    @pl.when(pl.program_id(0) == 0)
    def _():
        rows = iota((R, R), 0)
        rank = ((rows >> 1) & 1) * 32 + (rows & 1) * 16 + (rows >> 2)
        picked = dot(onehot(rank == iota((R, R), 1)), second_ref[...])
        swapped = jnp.concatenate([picked[:, CY:], picked[:, :CY]], axis=1)
        own = jnp.where(gy == 0, picked, swapped)
        weights_ref[...] = jnp.concatenate([own, own], axis=1).astype(bf16)

    weights = weights_ref[...]
    slot = iota((R, 128), 1) >> 5
    for ip in range(IPB):
        sides = []
        for s in range(2):
            keep_high, keep_low = split(keep_ref[s, ip])
            recv_high, recv_low = split(recv_ref[s, ip])
            sides.append(dot(weights, jnp.concatenate([keep_high, recv_high, keep_low, recv_low], axis=0)))
        for t in range(2):
            tiles = [sides[n // 2][:, n % 2 * 256 + t * 128 : n % 2 * 256 + (t + 1) * 128] for n in range(4)]
            for d in range(4):
                whole = tiles[0] if d == 0 else pltpu.roll(tiles[0], (128 - 32 * d) % 128, 1)
                for n in range(1, 4):
                    shift = 32 * (n - d) % 128
                    whole = jnp.where(slot == n, tiles[n] if shift == 0 else pltpu.roll(tiles[n], shift, 1), whole)
                for g in range(GX):
                    out_ref[4 * t + d, g, ip * 4 : ip * 4 + 4, :] = whole[4 * g : 4 * g + 4, :]


def local_projected(keep, recv, second):
    count = keep.shape[1]
    block = pl.BlockSpec((2, IPB, CY, 512), lambda i: (0, i, 0, 0))
    return pl.pallas_call(
        project_kernel,
        grid=(count // IPB,),
        in_specs=[block, block, pl.BlockSpec((R, 2 * CY), lambda i: (0, 0))],
        out_specs=pl.BlockSpec((GZ, GX, 4 * IPB, 128), lambda i: (0, 0, i, 0)),
        out_shape=jax.ShapeDtypeStruct((GZ, GX, 4 * count, 128), f32),
        scratch_shapes=[pltpu.VMEM((R, 4 * CY), bf16)],
        compiler_params=pltpu.CompilerParams(vmem_limit_bytes=40 * 2**20),
        cost_estimate=pl.CostEstimate(flops=count * 10**8, bytes_accessed=count * 700000, transcendentals=0),
        name="projected",
    )(keep, recv, second)


def gram_kernel(rows_ref, gram_ref, keep_ref, send_ref, columns_ref):
    gy = lax.axis_index("gy")
    low_lanes = iota((GX * HALF, 128), 1) < 64
    for t in range(2):
        first = rows_ref[pl.ds(2 * t, GX * HALF, stride=4), :]
        second = rows_ref[pl.ds(2 * t + 1, GX * HALF, stride=4), :]
        sides = (
            jnp.where(low_lanes, first, pltpu.roll(second, 64, 1)),
            jnp.where(low_lanes, pltpu.roll(first, 64, 1), second),
        )
        for s in range(2):
            for g in range(GX):
                top = g * CX + s * HALF
                columns_ref[top : top + HALF, t * 128 : (t + 1) * 128] = sides[s][g * HALF : (g + 1) * HALF, :]
    for n, (r, c) in enumerate(BLOCKS):
        gram_ref[n * 128 : (n + 1) * 128, :] = dot(
            columns_ref[r * 128 : (r + 1) * 128, :], columns_ref[c * 128 : (c + 1) * 128, :], (1, 1), highest
        )
    low, high = columns_ref[:, :128], columns_ref[:, 128:]
    keep_ref[...] = jnp.where(gy == 0, low, high)
    send_ref[...] = jnp.where(gy == 0, high, low)


def local_gram(rows):
    half = jax.ShapeDtypeStruct((NX, 128), f32)
    return pl.pallas_call(
        gram_kernel,
        out_shape=[jax.ShapeDtypeStruct((768, 128), f32), half, half],
        scratch_shapes=[pltpu.VMEM((NX, 256), f32)],
        name="gram",
    )(rows)


def split3(x):
    high = x.astype(bf16)
    rest = x - high.astype(f32)
    middle = rest.astype(bf16)
    return high, middle, (rest - middle.astype(f32)).astype(bf16)


def dot3(left, right, contract=(1, 0)):
    n = left[0].shape[0]
    all3 = dot(jnp.concatenate(left, axis=0), right[0], contract)
    two = dot(jnp.concatenate(left[:2], axis=0), right[1], contract)
    one = dot(left[0], right[2], contract)
    return all3[:n] + (all3[n : 2 * n] + two[:n]) + (all3[2 * n :] + two[n:] + one)


def invert_lower(matrix):
    row = iota((R, 128), 0)
    work = jnp.concatenate([matrix, jnp.where(iota((R, R), 0) == iota((R, R), 1), 1.0, 0.0)], axis=1)
    done = []
    for p in range(0, R, STEP):
        base = p // 8 * 8
        below = work[base:]
        columns = [jnp.broadcast_to(below[:, p + t : p + t + 1], below.shape) for t in range(STEP)]
        rows = [work[p + t : p + t + 1] for t in range(STEP)]
        for t in range(STEP):
            at = p + t - base
            pivot = columns[t][at : at + 1]
            inverse = 1.0 / pivot
            done.append(rows[t] * lax.rsqrt(pivot))
            scaled = rows[t] * inverse
            for s in range(t + 1, STEP):
                rows[s] = rows[s] - columns[t][p + s - base : p + s - base + 1] * scaled
                columns[s] = columns[s] - columns[t] * (columns[s][at : at + 1] * inverse)
            below = below - columns[t] * scaled
        work = below if base == 0 else jnp.concatenate([work[:base], below], axis=0)
    return jnp.concatenate(done, axis=0)[:, R:]


def factor_kernel(gram_ref, start_ref, keep_ref, recv_ref, factor_ref, core_ref, high_ref, middle_ref, low_ref):
    gy = lax.axis_index("gy")
    parts_refs = (high_ref, middle_ref, low_ref)
    for n, (r, c) in enumerate(BLOCKS):
        block = gram_ref[n * 128 : (n + 1) * 128, :]
        for ref, part in zip(parts_refs, split3(block)):
            ref[r * 128 : (r + 1) * 128, c * 128 : (c + 1) * 128] = part
        if r != c:
            for ref, part in zip(parts_refs, split3(block.T)):
                ref[c * 128 : (c + 1) * 128, r * 128 : (r + 1) * 128] = part
    gram = tuple(ref[...] for ref in parts_refs)
    basis = start_ref[...]
    for _ in range(SUB):
        product = dot3(split3(basis), gram)
        parts = split3(product)
        inner = dot3(parts, parts, (1, 1))
        basis = dot3(split3(invert_lower(inner)), parts)
    factor_ref[...] = basis
    keep, recv = keep_ref[...], recv_ref[...]
    low, high = jnp.where(gy == 0, keep, recv), jnp.where(gy == 0, recv, keep)
    low_lanes = iota((NX, 128), 1) < 64
    columns = (
        jnp.where(low_lanes, low, pltpu.roll(high, 64, 1)),
        jnp.where(low_lanes, pltpu.roll(low, 64, 1), high),
    )
    left = split(basis)
    for b in range(2):
        right = split(columns[b])
        both = dot(jnp.concatenate(left, axis=0), right[0])
        core = both[:R] + both[R:] + dot(left[0], right[1])
        for g in range(GX):
            core_ref[g, 4 * b : 4 * b + 4, :] = core[4 * g : 4 * g + 4, :]


def factor_and_core(gram, start, keep, recv):
    return pl.pallas_call(
        factor_kernel,
        out_shape=[jax.ShapeDtypeStruct((R, NX), f32), jax.ShapeDtypeStruct((GX, 8, 128), f32)],
        scratch_shapes=[pltpu.VMEM((NX, NX), bf16)] * 3,
        name="factor",
    )(gram, start, keep, recv)


def order_kernel(core_ref, out_ref, turned_ref):
    for a in range(4):
        pieces = [core_ref[pl.ds(4 * b + a, GX, stride=8), :] for b in range(2)]
        turned_ref[...] = jnp.concatenate(pieces, axis=0).T
        for c in range(8):
            out_ref[a, c] = turned_ref[pl.ds(c, RV, stride=8), :]


def ordered(core):
    out = pl.pallas_call(
        order_kernel,
        out_shape=jax.ShapeDtypeStruct((4, 8, RV, 32), f32),
        scratch_shapes=[pltpu.VMEM((128, 32), f32)],
        name="order",
    )(core.reshape(GX * 8, 128))
    return out.transpose(0, 3, 1, 2)


def swap(x):
    return lax.ppermute(x, "gy", [(0, 1), (1, 0)])


def exchange(x, axes):
    return lax.all_to_all(x, axes, 0, 0, tiled=True)


def per_device(field, start_first, factor_second, factor_third, factor_vars):
    field = field.reshape(V, 2, HALF, CY, CZ)
    sums = []
    first = 0
    for count in CHUNKS:
        keep, send = local_depth(field, factor_third.T, factor_vars.T, first, count)
        partial = local_projected(keep, swap(send), factor_second.T)
        sums.append(jnp.sum(exchange(partial, "gz"), axis=0))
        first += count
    rows = exchange(jnp.concatenate(sums, axis=1), "gx").reshape(GX * HALF * 4, 128)
    gram, keep, send = local_gram(rows)
    recv = swap(send)
    gram = jnp.sum(exchange(gram.reshape(16, 48, 128), ("gy", "gz")), axis=0)
    gram = jnp.sum(exchange(jnp.broadcast_to(gram, (16, 48, 128)), "gx"), axis=0)
    gram = exchange(jnp.broadcast_to(gram, (16, 48, 128)), ("gy", "gz")).reshape(768, 128)
    first_factor, core = factor_and_core(gram, start_first.T, keep, recv)
    return first_factor.T, ordered(exchange(core, "gx"))


def solution(mesh):
    in_specs = (P(None, "gx", "gy", "gz"), P(), P(), P(), P())
    out_specs = (P(), P("gx", "gy", "gz", None))
    return jax.shard_map(per_device, mesh=mesh, in_specs=in_specs, out_specs=out_specs, check_vma=False)
```

time: 185 us -> 171 us (0.924)
  blocking collectives: 99.8 us -> 67.4 us
  waiting for transfers between devices: 20 us -> 49.8 us
  Pallas kernels: 43.5 us -> 29.4 us
  starting transfers between devices: 9.47 us -> 14.4 us
  local copies, waits for them, and re-layouts: 10.7 us -> 6.81 us
    all_to_all x2 -> x3, waiting for transfers between devices: 15 us -> 48.7 us  [exchange(): return lax.all_to_all(x, axes, 0, 0, tiled=True)]
    all_to_all x4, blocking collectives: 99.8 us -> 67.4 us  [exchange(): return lax.all_to_all(x, axes, 0, 0, tiled=True)]
    pallas_call x3 -> x6, Pallas kernels: 40.8 us -> 26.7 us  [the longest x1 10.9 us: factor_and_core(): pl.pallas_call(factor_kernel, out_shape=[jax.ShapeDtypeStruct((R, NX), f3...]
    all_to_all x2 -> x3, starting transfers between devices: 8.79 us -> 13.2 us  [exchange(): return lax.all_to_all(x, axes, 0, 0, tiled=True)]
    ppermute x2 -> x3, waiting for transfers between devices: 5.02 us -> 1.11 us  [swap(): return lax.ppermute(x, 'gy', [(0, 1), (1, 0)])]
    reshape x2 -> x0, local copies, waits for them, and re-layouts: 2.06 us -> none  [the longest x1 1.49 us: per_device(): core = exchange(core.reshape(GX, 4, 256), 'gx')]
    unnamed x16 -> x14, local copies, waits for them, and re-layouts: 6.11 us -> 6.01 us
  transfers between devices with their start and end apart: 4 -> 6, of which waited for: 4 -> 4; matrix products, arithmetic and copies ran while one was open for 1% -> 1% of each run, Pallas kernels for 0% -> 7%
where the time goes in v2:
time: 171 us; the launch traced here: 170 us
  blocking collectives  67.4 us (39%)
  waiting for transfers between devices  49.8 us (29%)
  Pallas kernels  29.4 us (17%)
  starting transfers between devices  14.4 us (8%)
  local copies, waits for them, and re-layouts  6.81 us (4%)
    all_to_all x4, blocking collectives, exchange(): return lax.all_to_all(x, axes, 0, 0, tiled=True)  67.4 us
    all_to_all x3, waiting for transfers between devices, exchange(): return lax.all_to_all(x, axes, 0, 0, tiled=True)  48.7 us
    all_to_all x3, starting transfers between devices, exchange(): return lax.all_to_all(x, axes, 0, 0, tiled=True)  13.2 us
    pallas_call x1, Pallas kernels, factor_and_core(): pl.pallas_call(factor_kernel, out_shape=[jax.ShapeDtypeStruct((R, NX), f3...  10.9 us
    pallas_call x2, Pallas kernels, local_depth(): pl.pallas_call(depth_kernel, grid=(count // IPB,), in_specs=[pl.BlockSpec...  7.49 us
    pallas_call x2, Pallas kernels, local_projected(): pl.pallas_call(project_kernel, grid=(count // IPB,), in_specs=[block, blo...  6.66 us
    unnamed x14, local copies, waits for them, and re-layouts  6.01 us
  transfers between devices with their start and end apart: 6, of which 4 were waited for; matrix products, arithmetic and copies ran while one was open for 1% of the time, Pallas kernels for 7%

profile of v2, /device:TPU:2, one launch (start us, length us, event | category | flops | bytes accessed | tf_op | source)
XLA Modules:
  0.0 170.2 jit_solution(7084729446815550002)
XLA Ops:
  0.6 0.0 copy-start
  0.6 3.7 %copy-done = bf16[32,24,48,128]{3,2,1,0:T(8,128)(2,1)S(1)} copy-done((bf16[32,24,48,128]{3,2,1,0:T(8,128)(2,1)S(1)}, bf16[32,24,48,128]{3,2,1,0:T(8,128)(2,1)}, u32[]{:S(2)}) %copy-start) | copy-done | bytes 9437208
  4.3 0.0 copy-start.1
  4.3 0.9 copy-done.1
  5.2 0.0 copy-start.3
  5.2 0.7 copy-done.3
  5.9 2.4 %depth.2 = (f32[2,4,48,512]{3,2,1,0:T(8,128)S(1)}, f32[2,4,48,512]{3,2,1,0:T(8,128)S(1)}) custom-call(bf16[32,2,12,48,128]{4,3,2,1,0:T(8,128)(2,1)S(1)} %bitcast.11, bf16[64,1024]{1,0:T(8,128)(2,1)S(1)} %bitcast.13, bf16[16,32]{1,0:T(8,128)(2,1)S(1)} %bitcast.17), custom_call_target="tpu_custom_call" | custom-call | flops 2400000000 | bytes 4800000 | tf_op jit(solution)/shard_map/depth/pallas_call | solution.py:85
  8.3 0.0 copy-start.2
  8.3 0.1 collective-permute-start
  8.4 5.1 %depth.3 = (f32[2,8,48,512]{3,2,1,0:T(8,128)S(1)}, f32[2,8,48,512]{3,2,1,0:T(8,128)}) custom-call(bf16[32,2,12,48,128]{4,3,2,1,0:T(8,128)(2,1)S(1)} %bitcast.12, bf16[64,1024]{1,0:T(8,128)(2,1)S(1)} %bitcast.14, bf16[16,32]{1,0:T(8,128)(2,1)S(1)} %bitcast.18), custom_call_target="tpu_custom_call" | custom-call | flops 4800000000 | bytes 9600000 | tf_op jit(solution)/shard_map/depth/pallas_call | solution.py:85
  13.5 0.5 collective-permute-start.1
  14.0 0.0 collective-permute-done.recv_ref
  14.0 0.0 copy-done.2
  14.0 2.5 %projected.2 = f32[8,16,16,128]{3,2,1,0:T(8,128)} custom-call(f32[2,4,48,512]{3,2,1,0:T(8,128)S(1)} %get-tuple-element.11.keep_ref, f32[2,4,48,512]{3,2,1,0:T(8,128)S(1)} %collective-permute-done.recv_ref, bf16[64,96]{1,0:T(8,128)(2,1)S(1)} %bitcast.15), custom_call_target="tpu_custom_call" | custom-call | flops 400000000 | bytes 2800000 | tf_op jit(solution)/shard_map/projected/pallas_call | solution.py:145
  16.5 6.0 %all-to-all-start = ((f32[8,16,16,128]{3,2,1,0:T(8,128)}), f32[8,16,16,128]{3,2,1,0:T(8,128)}, u32[]{:S(2)}, u32[]{:S(2)}) async-start(f32[8,16,16,128]{3,2,1,0:T(8,128)} %projected.2), calls=%async_computation | async-start | bytes 2097152 | tf_op jit(solution)/shard_map/all_to_all | solution.py:295
  22.6 0.0 collective-permute-done.1.recv_ref
  22.6 4.1 %projected.3 = f32[8,16,32,128]{3,2,1,0:T(8,128)} custom-call(f32[2,8,48,512]{3,2,1,0:T(8,128)S(1)} %get-tuple-element.13.keep_ref, f32[2,8,48,512]{3,2,1,0:T(8,128)S(1)} %collective-permute-done.1.recv_ref, bf16[64,96]{1,0:T(8,128)(2,1)S(1)} %bitcast.16), custom_call_target="tpu_custom_call" | custom-call | flops 800000000 | bytes 5600000 | tf_op jit(solution)/shard_map/projected/pallas_call | solution.py:145
  26.7 13.4 %all-to-all-done = f32[8,16,16,128]{3,2,1,0:T(8,128)} async-done(((f32[8,16,16,128]{3,2,1,0:T(8,128)}), f32[8,16,16,128]{3,2,1,0:T(8,128)}, u32[]{:S(2)}, u32[]{:S(2)}) %all-to-all-start) | async-done | bytes 1048608 | tf_op jit(solution)/shard_map/all_to_all | solution.py:295
  40.1 3.6 %all-to-all-start.1 = ((f32[8,16,32,128]{3,2,1,0:T(8,128)}), f32[8,16,32,128]{3,2,1,0:T(8,128)S(1)}, u32[]{:S(2)}, u32[]{:S(2)}) async-start(f32[8,16,32,128]{3,2,1,0:T(8,128)} %projected.3), calls=%async_computation.1 | async-start | bytes 4194304 | tf_op jit(solution)/shard_map/all_to_all | solution.py:295
  43.7 1.3 reduce_sum.36
  45.0 26.4 %all-to-all-done.1 = f32[8,16,32,128]{3,2,1,0:T(8,128)S(1)} async-done(((f32[8,16,32,128]{3,2,1,0:T(8,128)}), f32[8,16,32,128]{3,2,1,0:T(8,128)S(1)}, u32[]{:S(2)}, u32[]{:S(2)}) %all-to-all-start.1) | async-done | bytes 2097184 | tf_op jit(solution)/shard_map/all_to_all | solution.py:295
  71.5 0.2 reduce_sum.37
  71.7 21.2 %all_to_all.35 = f32[16,48,128]{2,1,0:T(8,128)} all-to-all(f32[16,48,128]{2,1,0:T(8,128)S(1)} %pad_maximum_fusion), channel_id=1, replica_groups=mesh['gx'=16,'gy'=2,'gz'=8] {'gx'}, dimensions={0} | all-to-all | bytes 786432 | tf_op jit(solution)/shard_map/all_to_all | solution.py:295
  93.0 2.7 %gram.1 = (f32[768,128]{1,0:T(8,128)}, f32[384,128]{1,0:T(8,128)}, f32[384,128]{1,0:T(8,128)}) custom-call(f32[768,128]{1,0:T(8,128)} %bitcast.20), custom_call_target="tpu_custom_call" | custom-call | tf_op jit(solution)/shard_map/gram/pallas_call | solution.py:183
  95.7 0.0 copy-start.6
  95.7 15.4 %all_to_all.36 = f32[16,48,128]{2,1,0:T(8,128)S(1)} all-to-all(f32[16,48,128]{2,1,0:T(8,128)} %bitcast.21), channel_id=1, replica_groups=mesh['gx'=16,'gy'=2,'gz'=8] {'gy','gz'}, dimensions={0} | all-to-all | bytes 786432 | tf_op jit(solution)/shard_map/all_to_all | solution.py:295
  111.1 17.2 %all_to_all.37 = f32[16,48,128]{2,1,0:T(8,128)S(1)} all-to-all(f32[16,48,128]{2,1,0:T(8,128)S(1)} %broadcast_in_dim.6), channel_id=1, replica_groups=mesh['gx'=16,'gy'=2,'gz'=8] {'gx'}, dimensions={0} | all-to-all | bytes 786432 | tf_op jit(solution)/shard_map/all_to_all | solution.py:295
  128.3 0.8 broadcast_in_dim.7
  129.1 3.6 %all-to-all-start.5 = ((f32[16,48,128]{2,1,0:T(8,128)}), f32[16,48,128]{2,1,0:T(8,128)S(1)}, u32[]{:S(2)}, u32[]{:S(2)}) async-start(f32[16,48,128]{2,1,0:T(8,128)} %broadcast_in_dim.7), calls=%async_computation.5 | async-start | bytes 786432 | tf_op jit(solution)/shard_map/all_to_all | solution.py:295
  132.6 0.0 copy-done.6
  132.7 0.6 collective-permute-start.2
  133.3 1.1 collective-permute-done.2.recv_ref
  134.4 0.0 copy-start.5
  134.4 8.8 %all-to-all-done.5 = f32[16,48,128]{2,1,0:T(8,128)S(1)} async-done(((f32[16,48,128]{2,1,0:T(8,128)}), f32[16,48,128]{2,1,0:T(8,128)S(1)}, u32[]{:S(2)}, u32[]{:S(2)}) %all-to-all-start.5) | async-done | bytes 393248 | tf_op jit(solution)/shard_map/all_to_all | solution.py:295
  143.2 0.0 copy-start.4
  143.2 0.0 copy-done.5
  143.2 0.7 copy-done.4
  143.9 10.9 %factor.1 = (f32[64,384]{1,0:T(8,128)}, f32[16,8,128]{2,1,0:T(8,128)}) custom-call(f32[768,128]{1,0:T(8,128)} %bitcast.19, f32[64,384]{1,0:T(8,128)} %bitcast.24, f32[384,128]{1,0:T(8,128)} %get-tuple-element.16.keep_ref, f32[384,128]{1,0:T(8,128)} %copy-done.5), custom_call_target="tpu_custom_call" | custom-call | tf_op jit(solution)/shard_map/factor/pallas_call | solution.py:264
  154.8 13.6 %all_to_all.38 = f32[16,8,128]{2,1,0:T(8,128)} all-to-all(f32[16,8,128]{2,1,0:T(8,128)} %get-tuple-element.19), channel_id=1, replica_groups=mesh['gx'=16,'gy'=2,'gz'=8] {'gx'}, dimensions={0} | all-to-all | bytes 131072 | tf_op jit(solution)/shard_map/all_to_all | solution.py:295
  168.5 1.7 %order.1 = f32[4,8,16,32]{3,2,1,0:T(8,128)} custom-call(f32[128,128]{1,0:T(8,128)} %bitcast.23), custom_call_target="tpu_custom_call" | custom-call | tf_op jit(solution)/shard_map/order/pallas_call | solution.py:281
  (4 shorter events, 0.1 us)
Async XLA Ops:
  0.6 3.7 %copy-start = (bf16[32,24,48,128]{3,2,1,0:T(8,128)(2,1)S(1)}, bf16[32,24,48,128]{3,2,1,0:T(8,128)(2,1)}, u32[]{:S(2)}) copy-start(bf16[32,24,48,128]{3,2,1,0:T(8,128)(2,1)} %param.5) | copy-start | bytes 28311556
  4.3 0.9 copy-start.1
  5.2 0.7 copy-start.3
  8.3 5.7 %copy-start.2 = (bf16[96,64]{0,1:T(8,128)(2,1)S(1)}, bf16[96,64]{0,1:T(8,128)(2,1)}, u32[]{:S(2)}) copy-start(bf16[96,64]{0,1:T(8,128)(2,1)} %param.7) | copy-start | bytes 36868
  8.3 5.7 %collective-permute-start = (f32[2,4,48,512]{3,2,1,0:T(8,128)S(1)}, f32[2,4,48,512]{3,2,1,0:T(8,128)S(1)}, u32[]{:S(2)}, u32[]{:S(2)}) collective-permute-start(f32[2,4,48,512]{3,2,1,0:T(8,128)S(1)} %get-tuple-element.12), channel_id=1, source_target_pairs={{0,8},{8,0},{1,9},{9,1},{2,10},{10,2},{3,11},{11,3},{4,12},{12,4},... | collective-permute-start | bytes 2359304 | tf_op jit(solution)/shard_map/ppermute | solution.py:291
  13.5 9.1 %collective-permute-start.1 = (f32[2,8,48,512]{3,2,1,0:T(8,128)}, f32[2,8,48,512]{3,2,1,0:T(8,128)S(1)}, u32[]{:S(2)}, u32[]{:S(2)}) collective-permute-start(f32[2,8,48,512]{3,2,1,0:T(8,128)} %get-tuple-element.14), channel_id=1, source_target_pairs={{0,8},{8,0},{1,9},{9,1},{2,10},{10,2},{3,11},{11,3},{4,12},{12,4},... | collective-permute-start | bytes 4718600 | tf_op jit(solution)/shard_map/ppermute | solution.py:291
  16.5 23.6 %all-to-all-start = ((f32[8,16,16,128]{3,2,1,0:T(8,128)}), f32[8,16,16,128]{3,2,1,0:T(8,128)}, u32[]{:S(2)}, u32[]{:S(2)}) async-start(f32[8,16,16,128]{3,2,1,0:T(8,128)} %projected.2), calls=%async_computation | async-start | bytes 2097152 | tf_op jit(solution)/shard_map/all_to_all | solution.py:295
  40.1 31.4 %all-to-all-start.1 = ((f32[8,16,32,128]{3,2,1,0:T(8,128)}), f32[8,16,32,128]{3,2,1,0:T(8,128)S(1)}, u32[]{:S(2)}, u32[]{:S(2)}) async-start(f32[8,16,32,128]{3,2,1,0:T(8,128)} %projected.3), calls=%async_computation.1 | async-start | bytes 4194304 | tf_op jit(solution)/shard_map/all_to_all | solution.py:295
  95.7 37.0 %copy-start.6 = (f32[384,128]{1,0:T(8,128)S(1)}, f32[384,128]{1,0:T(8,128)}, u32[]{:S(2)}) copy-start(f32[384,128]{1,0:T(8,128)} %get-tuple-element.17) | copy-start | bytes 589828
  129.1 14.1 %all-to-all-start.5 = ((f32[16,48,128]{2,1,0:T(8,128)}), f32[16,48,128]{2,1,0:T(8,128)S(1)}, u32[]{:S(2)}, u32[]{:S(2)}) async-start(f32[16,48,128]{2,1,0:T(8,128)} %broadcast_in_dim.7), calls=%async_computation.5 | async-start | bytes 786432 | tf_op jit(solution)/shard_map/all_to_all | solution.py:295
  132.7 1.7 %collective-permute-start.2 = (f32[384,128]{1,0:T(8,128)S(1)}, f32[384,128]{1,0:T(8,128)S(1)}, u32[]{:S(2)}, u32[]{:S(2)}) collective-permute-start(f32[384,128]{1,0:T(8,128)S(1)} %copy-done.6), channel_id=1, source_target_pairs={{0,8},{8,0},{1,9},{9,1},{2,10},{10,2},{3,11},{11,3},{4,12},{12,4},... | collective-permute-start | bytes 589832 | tf_op jit(solution)/shard_map/ppermute | solution.py:291
  134.4 8.9 %copy-start.5 = (f32[384,128]{1,0:T(8,128)}, f32[384,128]{1,0:T(8,128)S(1)}, u32[]{:S(2)}) copy-start(f32[384,128]{1,0:T(8,128)S(1)} %collective-permute-done.2.recv_ref) | copy-start | bytes 589828
  143.2 0.7 copy-start.4

commit v3 on v2

--- a/solution.py
+++ b/solution.py
@@ -17,9 +17,8 @@
 HALF = CX // 2
 EH = RV // 2
 NX = 384
-IPB = 2
-STEP = 4
-CHUNKS = (4, 8)
+IPB = 4
+STEP = 16
 BLOCKS = ((0, 0), (0, 1), (0, 2), (1, 1), (1, 2), (2, 2))
 
 f32 = jnp.float32
@@ -41,66 +40,87 @@
     )
 
 
-def depth_kernel(field_ref, third_ref, vars_ref, keep_ref, send_ref, mix_ref, cols_ref, left_ref):
+def depth_kernel(
+    field_ref, third_ref, vars_ref, keep_ref, send_ref, cells_ref, third_here, vars_here, mix_ref, cols_ref, left_ref, sems
+):
     gy = lax.axis_index("gy")
     gz = lax.axis_index("gz")
 
-    @pl.when(pl.program_id(0) == 0)
-    def _():
-        rows = iota((256, RV), 0)
-        pick_e = onehot((((rows >> 4) + EH * gy) & (RV - 1)) == iota((256, RV), 1))
-        wide = dot(pick_e, vars_ref[...]).astype(bf16)
-        spread = onehot(iota((V, 512), 0) == iota((V, 512), 1) >> 4)
-        same_j = (iota((256, 512), 0) & 15) == (iota((256, 512), 1) & 15)
-        mix_ref[...] = jnp.where(same_j, dot(wide, spread), 0.0).astype(bf16)
-        third = third_ref[:, pl.ds(pl.multiple_of(gz * CZ, CZ), CZ)]
-        lane = iota((R, 256), 1)
-        spread = onehot(iota((R, 256), 0) == (lane >> 5) * 8 + (lane & 7))
-        full = dot(third, spread, (0, 0))
-        which = (iota((CZ, 256), 1) >> 3) & 3
-        for e in range(4):
-            cols_ref[e * CZ : (e + 1) * CZ, :] = jnp.where(which == e, full, 0.0).astype(bf16)
-
-    mix = mix_ref[...]
-    for ip in range(IPB):
-        for jb in range(CY // 16):
-            pieces = [field_ref[:, s, ip, jb * 16 : jb * 16 + 16, :].reshape(512, CZ) for s in range(2)]
-            reduced = dot(mix, jnp.concatenate(pieces, axis=1)).astype(bf16)
-            for e in range(RV):
-                for s in range(2):
-                    top = ((e // 4 * 2 + s) * IPB + ip) * CY + jb * 16
-                    left_ref[top : top + 16, e % 4 * CZ : (e % 4 + 1) * CZ] = reduced[
-                        e * 16 : e * 16 + 16, s * CZ : (s + 1) * CZ
-                    ]
-    cols = cols_ref[...]
-    size = 2 * IPB * CY
-    for n in range(4):
-        depth = dot(left_ref[n * size : (n + 1) * size, :], cols).reshape(2, IPB, CY, 256)
-        (keep_ref, send_ref)[n // 2][:, :, :, n % 2 * 256 : (n % 2 + 1) * 256] = depth
-
-
-def local_depth(field, third, weights, first, count):
-    half = jax.ShapeDtypeStruct((2, count, CY, 512), f32)
-    block = pl.BlockSpec((2, IPB, CY, 512), lambda i: (0, i, 0, 0))
+    def fetch(chunk):
+        cells = pl.ds(chunk * IPB, IPB)
+        return pltpu.make_async_copy(field_ref.at[:, :, cells], cells_ref.at[:, :, cells], sems.at[chunk])
+
+    third_part = third_ref.at[:, pl.ds(pl.multiple_of(gz * CZ, CZ), CZ)]
+    third_copy = pltpu.make_async_copy(third_part, third_here, sems.at[HALF // IPB])
+    vars_copy = pltpu.make_async_copy(vars_ref, vars_here, sems.at[HALF // IPB + 1])
+    third_copy.start()
+    vars_copy.start()
+    for chunk in range(HALF // IPB):
+        fetch(chunk).start()
+
+    rows = iota((128, RV), 0)
+    pick_e = onehot((((rows >> 3) + EH * gy) & (RV - 1)) == iota((128, RV), 1))
+    vars_copy.wait()
+    wide = dot(pick_e, vars_here[...]).astype(bf16)
+    spread = onehot(iota((V, 256), 0) == iota((V, 256), 1) >> 3)
+    same_j = (iota((128, 256), 0) & 7) == (iota((128, 256), 1) & 7)
+    mix_ref[...] = jnp.where(same_j, dot(wide, spread), 0.0).astype(bf16)
+    lane = iota((R, 256), 1)
+    spread = onehot(iota((R, 256), 0) == (lane >> 5) * 8 + (lane & 7))
+    third_copy.wait()
+    full = dot(third_here[...], spread, (0, 0))
+    which = (iota((CZ, 256), 1) >> 3) & 3
+    for e in range(4):
+        cols_ref[e * CZ : (e + 1) * CZ, :] = jnp.where(which == e, full, 0.0).astype(bf16)
+
+    def step(chunk, carry):
+        fetch(chunk).wait()
+        mix = mix_ref[...]
+        for ip in range(IPB):
+            for jb in range(CY // 16):
+                tiles = [cells_ref[:, s, chunk * IPB + ip, jb * 16 : jb * 16 + 16, :] for s in range(2)]
+                halves = []
+                for h in range(2):
+                    pieces = [tile[:, h * 8 : h * 8 + 8, :].reshape(256, CZ) for tile in tiles]
+                    halves.append(dot(mix, jnp.concatenate(pieces, axis=1)).reshape(RV, 8, 2 * CZ))
+                reduced = jnp.concatenate(halves, axis=1).astype(bf16)
+                for e in range(RV):
+                    for s in range(2):
+                        top = ((e // 4 * 2 + s) * IPB + ip) * CY + jb * 16
+                        left_ref[chunk % 2, top : top + 16, e % 4 * CZ : (e % 4 + 1) * CZ] = reduced[
+                            e, :, s * CZ : (s + 1) * CZ
+                        ]
+        depth = dot(left_ref[chunk % 2], cols_ref[...]).reshape(4, 2, IPB, CY, 256)
+        for n in range(4):
+            half = (keep_ref, send_ref)[n // 2]
+            half[:, pl.ds(chunk * IPB, IPB), :, n % 2 * 256 : (n % 2 + 1) * 256] = depth[n]
+        return carry
+
+    lax.fori_loop(0, HALF // IPB, step, 0)
+
+
+def local_depth(field, third, weights):
+    half = jax.ShapeDtypeStruct((2, HALF, CY, 512), f32)
+    far = pl.BlockSpec(memory_space=pltpu.HBM)
+    near = pl.BlockSpec(memory_space=pltpu.VMEM)
     return pl.pallas_call(
         depth_kernel,
-        grid=(count // IPB,),
-        in_specs=[
-            pl.BlockSpec((V, 2, IPB, CY, CZ), lambda i: (0, 0, i + first // IPB, 0, 0)),
-            pl.BlockSpec((R, 1024), lambda i: (0, 0)),
-            pl.BlockSpec((RV, V), lambda i: (0, 0)),
-        ],
-        out_specs=[block, block],
+        in_specs=[far, far, far],
+        out_specs=[near, near],
         out_shape=[half, half],
         scratch_shapes=[
-            pltpu.VMEM((256, 512), bf16),
+            pltpu.VMEM((V, 2, HALF, CY, CZ), bf16),
+            pltpu.VMEM((R, CZ), bf16),
+            pltpu.VMEM((RV, V), bf16),
+            pltpu.VMEM((128, 256), bf16),
             pltpu.VMEM((512, 256), bf16),
-            pltpu.VMEM((8 * IPB * CY, 512), bf16),
+            pltpu.VMEM((2, 8 * IPB * CY, 512), bf16),
+            pltpu.SemaphoreType.DMA((HALF // IPB + 2,)),
         ],
-        compiler_params=pltpu.CompilerParams(vmem_limit_bytes=40 * 2**20),
-        cost_estimate=pl.CostEstimate(flops=count * 6 * 10**8, bytes_accessed=count * 1200000, transcendentals=0),
+        compiler_params=pltpu.CompilerParams(vmem_limit_bytes=28 * 2**20),
+        cost_estimate=pl.CostEstimate(flops=7 * 10**9, bytes_accessed=14 * 2**20, transcendentals=0),
         name="depth",
-    )(field, third, weights)
+    )(*(pltpu.with_memory_space_constraint(x, pltpu.HBM) for x in (field, third, weights)))
 
 
 def split(x):
@@ -108,21 +128,33 @@
     return high, (x - high.astype(f32)).astype(bf16)
 
 
-def project_kernel(keep_ref, recv_ref, second_ref, out_ref, weights_ref):
+def turn_lanes(tiles, slot):
+    skewed = []
+    for k in range(4):
+        mixed = tiles[-k % 4]
+        for q in range(1, 4):
+            mixed = jnp.where(slot == q, tiles[(q - k) % 4], mixed)
+        skewed.append(mixed if k == 0 else pltpu.roll(mixed, 128 - 32 * k, 1))
+    turned = []
+    for d in range(4):
+        whole = skewed[d]
+        for n in range(1, 4):
+            whole = jnp.where(slot == n, skewed[(d - n) % 4], whole)
+        turned.append(whole)
+    return turned
+
+
+def project_kernel(keep_ref, recv_ref, second_ref, out_ref):
     gy = lax.axis_index("gy")
-
-    @pl.when(pl.program_id(0) == 0)
-    def _():
-        rows = iota((R, R), 0)
-        rank = ((rows >> 1) & 1) * 32 + (rows & 1) * 16 + (rows >> 2)
-        picked = dot(onehot(rank == iota((R, R), 1)), second_ref[...])
-        swapped = jnp.concatenate([picked[:, CY:], picked[:, :CY]], axis=1)
-        own = jnp.where(gy == 0, picked, swapped)
-        weights_ref[...] = jnp.concatenate([own, own], axis=1).astype(bf16)
-
-    weights = weights_ref[...]
+    rows = iota((R, R), 0)
+    rank = ((rows >> 1) & 1) * 32 + (rows & 1) * 16 + (rows >> 2)
+    picked = dot(onehot(rank == iota((R, R), 1)), second_ref[...])
+    swapped = jnp.concatenate([picked[:, CY:], picked[:, :CY]], axis=1)
+    own = jnp.where(gy == 0, picked, swapped)
+    weights = jnp.concatenate([own, own], axis=1).astype(bf16)
     slot = iota((R, 128), 1) >> 5
-    for ip in range(IPB):
+
+    def step(ip, carry):
         sides = []
         for s in range(2):
             keep_high, keep_low = split(keep_ref[s, ip])
@@ -130,27 +162,19 @@
             sides.append(dot(weights, jnp.concatenate([keep_high, recv_high, keep_low, recv_low], axis=0)))
         for t in range(2):
             tiles = [sides[n // 2][:, n % 2 * 256 + t * 128 : n % 2 * 256 + (t + 1) * 128] for n in range(4)]
-            for d in range(4):
-                whole = tiles[0] if d == 0 else pltpu.roll(tiles[0], (128 - 32 * d) % 128, 1)
-                for n in range(1, 4):
-                    shift = 32 * (n - d) % 128
-                    whole = jnp.where(slot == n, tiles[n] if shift == 0 else pltpu.roll(tiles[n], shift, 1), whole)
-                for g in range(GX):
-                    out_ref[4 * t + d, g, ip * 4 : ip * 4 + 4, :] = whole[4 * g : 4 * g + 4, :]
+            for d, tile in enumerate(turn_lanes(tiles, slot)):
+                out_ref[4 * t + d, ip] = tile
+        return carry
+
+    lax.fori_loop(0, HALF, step, 0, unroll=3)
 
 
 def local_projected(keep, recv, second):
-    count = keep.shape[1]
-    block = pl.BlockSpec((2, IPB, CY, 512), lambda i: (0, i, 0, 0))
     return pl.pallas_call(
         project_kernel,
-        grid=(count // IPB,),
-        in_specs=[block, block, pl.BlockSpec((R, 2 * CY), lambda i: (0, 0))],
-        out_specs=pl.BlockSpec((GZ, GX, 4 * IPB, 128), lambda i: (0, 0, i, 0)),
-        out_shape=jax.ShapeDtypeStruct((GZ, GX, 4 * count, 128), f32),
-        scratch_shapes=[pltpu.VMEM((R, 4 * CY), bf16)],
-        compiler_params=pltpu.CompilerParams(vmem_limit_bytes=40 * 2**20),
-        cost_estimate=pl.CostEstimate(flops=count * 10**8, bytes_accessed=count * 700000, transcendentals=0),
+        out_shape=jax.ShapeDtypeStruct((GZ, HALF, R, 128), f32),
+        compiler_params=pltpu.CompilerParams(vmem_limit_bytes=16 * 2**20),
+        cost_estimate=pl.CostEstimate(flops=10**9, bytes_accessed=8 * 2**20, transcendentals=0),
         name="projected",
     )(keep, recv, second)
 
@@ -169,10 +193,11 @@
             for g in range(GX):
                 top = g * CX + s * HALF
                 columns_ref[top : top + HALF, t * 128 : (t + 1) * 128] = sides[s][g * HALF : (g + 1) * HALF, :]
+    parts = split3(columns_ref[...])
     for n, (r, c) in enumerate(BLOCKS):
-        gram_ref[n * 128 : (n + 1) * 128, :] = dot(
-            columns_ref[r * 128 : (r + 1) * 128, :], columns_ref[c * 128 : (c + 1) * 128, :], (1, 1), highest
-        )
+        left = [part[r * 128 : (r + 1) * 128, :] for part in parts]
+        right = [part[c * 128 : (c + 1) * 128, :] for part in parts]
+        gram_ref[n * 128 : (n + 1) * 128, :] = dot3(left, right, (1, 1))
     low, high = columns_ref[:, :128], columns_ref[:, 128:]
     keep_ref[...] = jnp.where(gy == 0, low, high)
     send_ref[...] = jnp.where(gy == 0, high, low)
@@ -184,6 +209,7 @@
         gram_kernel,
         out_shape=[jax.ShapeDtypeStruct((768, 128), f32), half, half],
         scratch_shapes=[pltpu.VMEM((NX, 256), f32)],
+        compiler_params=pltpu.CompilerParams(vmem_limit_bytes=8 * 2**20),
         name="gram",
     )(rows)
 
@@ -265,6 +291,7 @@
         factor_kernel,
         out_shape=[jax.ShapeDtypeStruct((R, NX), f32), jax.ShapeDtypeStruct((GX, 8, 128), f32)],
         scratch_shapes=[pltpu.VMEM((NX, NX), bf16)] * 3,
+        compiler_params=pltpu.CompilerParams(vmem_limit_bytes=8 * 2**20),
         name="factor",
     )(gram, start, keep, recv)
 
@@ -282,6 +309,7 @@
         order_kernel,
         out_shape=jax.ShapeDtypeStruct((4, 8, RV, 32), f32),
         scratch_shapes=[pltpu.VMEM((128, 32), f32)],
+        compiler_params=pltpu.CompilerParams(vmem_limit_bytes=8 * 2**20),
         name="order",
     )(core.reshape(GX * 8, 128))
     return out.transpose(0, 3, 1, 2)
@@ -297,14 +325,11 @@
 
 def per_device(field, start_first, factor_second, factor_third, factor_vars):
     field = field.reshape(V, 2, HALF, CY, CZ)
-    sums = []
-    first = 0
-    for count in CHUNKS:
-        keep, send = local_depth(field, factor_third.T, factor_vars.T, first, count)
-        partial = local_projected(keep, swap(send), factor_second.T)
-        sums.append(jnp.sum(exchange(partial, "gz"), axis=0))
-        first += count
-    rows = exchange(jnp.concatenate(sums, axis=1), "gx").reshape(GX * HALF * 4, 128)
+    keep, send = local_depth(field, factor_third.T, factor_vars.T)
+    partial = local_projected(keep, swap(send), factor_second.T)
+    projected = jnp.sum(exchange(partial, "gz"), axis=0)
+    projected = projected.reshape(HALF, GX, 4, 128).transpose(1, 0, 2, 3).reshape(GX, HALF * 4, 128)
+    rows = exchange(projected, "gx").reshape(GX * HALF * 4, 128)
     gram, keep, send = local_gram(rows)
     recv = swap(send)
     gram = jnp.sum(exchange(gram.reshape(16, 48, 128), ("gy", "gz")), axis=0)

time: 171 us -> 149 us (0.87)
  blocking collectives: 67.4 us -> 111 us
  waiting for transfers between devices: 49.8 us -> 14.8 us
  Pallas kernels: 29.4 us -> 16.7 us
  starting transfers between devices: 14.4 us -> 4.21 us
  local copies, waits for them, and re-layouts: 6.81 us -> 0.95 us
    all_to_all x4 -> x5, blocking collectives: 67.4 us -> 111 us  [exchange(): return lax.all_to_all(x, axes, 0, 0, tiled=True)]
    all_to_all x3 -> x1, waiting for transfers between devices: 48.7 us -> 9.14 us  [exchange(): return lax.all_to_all(x, axes, 0, 0, tiled=True)]
    all_to_all x3 -> x1, starting transfers between devices: 13.2 us -> 3.71 us  [exchange(): return lax.all_to_all(x, axes, 0, 0, tiled=True)]
    pallas_call x4 -> x2, Pallas kernels: 14.1 us -> 7.52 us  [the longest x1 5.39 us: local_depth(): pl.pallas_call(depth_kernel, in_specs=[far, far, far], out_specs=[near, n...]
    unnamed x14 -> x4, local copies, waits for them, and re-layouts: 6.01 us -> 0.01 us
    ppermute x3 -> x2, waiting for transfers between devices: 1.11 us -> 5.64 us  [swap(): return lax.ppermute(x, 'gy', [(0, 1), (1, 0)])]
    pallas_call x1, Pallas kernels: 10.9 us -> 7.41 us  [factor_and_core(): pl.pallas_call(factor_kernel, out_shape=[jax.ShapeDtypeStruct((R, NX), f3...]
    pallas_call x1, Pallas kernels: 2.7 us -> 0.93 us  [local_gram(): pl.pallas_call(gram_kernel, out_shape=[jax.ShapeDtypeStruct((768, 128), f...]
  transfers between devices with their start and end apart: 6 -> 3, of which waited for: 4 -> 3; matrix products, arithmetic and copies ran while one was open for 1% -> 0% of each run, Pallas kernels for 7% -> 0%
where the time goes in v3:
time: 149 us
  blocking collectives  111 us (74%)
  Pallas kernels  16.7 us (11%)
  waiting for transfers between devices  14.8 us (10%)
  starting transfers between devices  4.21 us (3%)
    all_to_all x5, blocking collectives, exchange(): return lax.all_to_all(x, axes, 0, 0, tiled=True)  111 us
    all_to_all x1, waiting for transfers between devices, exchange(): return lax.all_to_all(x, axes, 0, 0, tiled=True)  9.14 us
    pallas_call x1, Pallas kernels, factor_and_core(): pl.pallas_call(factor_kernel, out_shape=[jax.ShapeDtypeStruct((R, NX), f3...  7.41 us
    ppermute x2, waiting for transfers between devices, swap(): return lax.ppermute(x, 'gy', [(0, 1), (1, 0)])  5.64 us
    pallas_call x1, Pallas kernels, local_depth(): pl.pallas_call(depth_kernel, in_specs=[far, far, far], out_specs=[near, n...  5.39 us
    all_to_all x1, starting transfers between devices, exchange(): return lax.all_to_all(x, axes, 0, 0, tiled=True)  3.71 us
  transfers between devices with their start and end apart: 3, of which 3 were waited for; matrix products, arithmetic and copies ran while one was open for 0% of the time, Pallas kernels for 0%

profile of v3, /device:TPU:2, one launch (start us, length us, event | category | flops | bytes accessed | tf_op | source)
XLA Modules:
  0.0 148.7 jit_solution(10324587791896695038)
XLA Ops:
  0.6 0.0 copy-start.1
  0.6 5.4 %depth.1 = (f32[2,12,48,512]{3,2,1,0:T(8,128)S(1)}, f32[2,12,48,512]{3,2,1,0:T(8,128)S(1)}) custom-call(bf16[32,2,12,48,128]{4,3,2,1,0:T(8,128)(2,1)} %bitcast.24, bf16[64,1024]{1,0:T(8,128)(2,1)} %bitcast.25, bf16[16,32]{1,0:T(8,128)(2,1)} %bitcast.27), custom_call_target="tpu_custom_call" | custom-call | flops 7000000000 | bytes 14680064 | tf_op jit(solution)/shard_map/depth/pallas_call | solution.py:106
  6.0 0.1 collective-permute-start
  6.1 4.5 %collective-permute-done.recv_ref = f32[2,12,48,512]{3,2,1,0:T(8,128)S(1)} collective-permute-done((f32[2,12,48,512]{3,2,1,0:T(8,128)S(1)}, f32[2,12,48,512]{3,2,1,0:T(8,128)S(1)}, u32[]{:S(2)}, u32[]{:S(2)}) %collective-permute-start) | collective-permute-done | bytes 2359328 | tf_op jit(solution)/shard_map/ppermute | solution.py:319
  10.7 0.0 copy-done.1
  10.7 2.1 %projected.1 = f32[8,12,64,128]{3,2,1,0:T(8,128)S(1)} custom-call(f32[2,12,48,512]{3,2,1,0:T(8,128)S(1)} %get-tuple-element.9.keep_ref, f32[2,12,48,512]{3,2,1,0:T(8,128)S(1)} %collective-permute-done.recv_ref, bf16[64,96]{1,0:T(8,128)(2,1)S(1)} %bitcast.20), custom_call_target="tpu_custom_call" | custom-call | flops 1000000000 | bytes 8388608 | tf_op jit(solution)/shard_map/projected/pallas_call | solution.py:173
  12.8 45.8 %all_to_all.30 = f32[8,12,64,128]{3,2,1,0:T(8,128)S(1)} all-to-all(f32[8,12,64,128]{3,2,1,0:T(8,128)S(1)} %projected.1), channel_id=1, replica_groups=mesh['gx'=16,'gy'=2,'gz'=8] {'gz'}, dimensions={0} | all-to-all | bytes 6291456 | tf_op jit(solution)/shard_map/all_to_all | solution.py:323
  58.6 0.3 reduce_sum.27
  58.9 0.0 copy-start
  58.9 0.1 copy.12
  59.1 21.9 %all_to_all.31 = f32[16,48,128]{2,1,0:T(8,128)S(1)} all-to-all(f32[16,48,128]{2,1,0:T(8,128)S(1)} %copy.12), channel_id=1, replica_groups=mesh['gx'=16,'gy'=2,'gz'=8] {'gx'}, dimensions={0} | all-to-all | bytes 786432 | tf_op jit(solution)/shard_map/all_to_all | solution.py:323
  81.0 0.9 gram.1
  81.9 13.7 %all_to_all.32 = f32[16,48,128]{2,1,0:T(8,128)S(1)} all-to-all(f32[16,48,128]{2,1,0:T(8,128)S(1)} %bitcast.17), channel_id=1, replica_groups=mesh['gx'=16,'gy'=2,'gz'=8] {'gy','gz'}, dimensions={0} | all-to-all | bytes 786432 | tf_op jit(solution)/shard_map/all_to_all | solution.py:323
  95.7 17.6 %all_to_all.33 = f32[16,48,128]{2,1,0:T(8,128)S(1)} all-to-all(f32[16,48,128]{2,1,0:T(8,128)S(1)} %broadcast_in_dim.6), channel_id=1, replica_groups=mesh['gx'=16,'gy'=2,'gz'=8] {'gx'}, dimensions={0} | all-to-all | bytes 786432 | tf_op jit(solution)/shard_map/all_to_all | solution.py:323
  113.3 0.8 broadcast_in_dim.7
  114.1 3.7 %all-to-all-start.4 = ((f32[16,48,128]{2,1,0:T(8,128)}), f32[16,48,128]{2,1,0:T(8,128)S(1)}, u32[]{:S(2)}, u32[]{:S(2)}) async-start(f32[16,48,128]{2,1,0:T(8,128)} %broadcast_in_dim.7), calls=%async_computation.4 | async-start | bytes 786432 | tf_op jit(solution)/shard_map/all_to_all | solution.py:323
  117.8 0.4 collective-permute-start.1
  118.2 1.1 collective-permute-done.1.recv_ref
  119.3 9.1 %all-to-all-done.4 = f32[16,48,128]{2,1,0:T(8,128)S(1)} async-done(((f32[16,48,128]{2,1,0:T(8,128)}), f32[16,48,128]{2,1,0:T(8,128)S(1)}, u32[]{:S(2)}, u32[]{:S(2)}) %all-to-all-start.4) | async-done | bytes 393248 | tf_op jit(solution)/shard_map/all_to_all | solution.py:323
  128.5 0.0 copy-done
  128.5 7.4 %factor.1 = (f32[64,384]{1,0:T(8,128)}, f32[16,8,128]{2,1,0:T(8,128)S(1)}) custom-call(f32[768,128]{1,0:T(8,128)S(1)} %bitcast.15, f32[64,384]{1,0:T(8,128)S(1)} %bitcast.19, f32[384,128]{1,0:T(8,128)S(1)} %get-tuple-element.12.keep_ref, f32[384,128]{1,0:T(8,128)S(1)} %collective-permute-done.1.recv_ref), custom_call_target="tpu_custom_call" | custom-call | tf_op jit(solution)/shard_map/factor/pallas_call | solution.py:290
  135.9 12.0 %all_to_all.34 = f32[16,8,128]{2,1,0:T(8,128)S(1)} all-to-all(f32[16,8,128]{2,1,0:T(8,128)S(1)} %get-tuple-element.15), channel_id=1, replica_groups=mesh['gx'=16,'gy'=2,'gz'=8] {'gx'}, dimensions={0} | all-to-all | bytes 131072 | tf_op jit(solution)/shard_map/all_to_all | solution.py:323
  147.9 0.9 order.1
  (4 shorter events, 0.1 us)
Async XLA Ops:
  0.6 10.0 %copy-start.1 = (bf16[96,64]{0,1:T(8,128)(2,1)S(1)}, bf16[96,64]{0,1:T(8,128)(2,1)}, u32[]{:S(2)}) copy-start(bf16[96,64]{0,1:T(8,128)(2,1)} %param.7) | copy-start | bytes 36868
  6.0 4.6 %collective-permute-start = (f32[2,12,48,512]{3,2,1,0:T(8,128)S(1)}, f32[2,12,48,512]{3,2,1,0:T(8,128)S(1)}, u32[]{:S(2)}, u32[]{:S(2)}) collective-permute-start(f32[2,12,48,512]{3,2,1,0:T(8,128)S(1)} %get-tuple-element.10), channel_id=1, source_target_pairs={{0,8},{8,0},{1,9},{9,1},{2,10},{10,2},{3,11},{11,3},{4,12},{12,4},... | collective-permute-start | bytes 7077896 | tf_op jit(solution)/shard_map/ppermute | solution.py:319
  58.9 69.6 %copy-start = (f32[384,64]{0,1:T(8,128)S(1)}, f32[384,64]{0,1:T(8,128)}, u32[]{:S(2)}) copy-start(f32[384,64]{0,1:T(8,128)} %param.6) | copy-start | bytes 294916
  114.1 14.4 %all-to-all-start.4 = ((f32[16,48,128]{2,1,0:T(8,128)}), f32[16,48,128]{2,1,0:T(8,128)S(1)}, u32[]{:S(2)}, u32[]{:S(2)}) async-start(f32[16,48,128]{2,1,0:T(8,128)} %broadcast_in_dim.7), calls=%async_computation.4 | async-start | bytes 786432 | tf_op jit(solution)/shard_map/all_to_all | solution.py:323
  117.8 1.5 %collective-permute-start.1 = (f32[384,128]{1,0:T(8,128)S(1)}, f32[384,128]{1,0:T(8,128)S(1)}, u32[]{:S(2)}, u32[]{:S(2)}) collective-permute-start(f32[384,128]{1,0:T(8,128)S(1)} %get-tuple-element.13), channel_id=1, source_target_pairs={{0,8},{8,0},{1,9},{9,1},{2,10},{10,2},{3,11},{11,3},{4,12},{12,4},... | collective-permute-start | bytes 589832 | tf_op jit(solution)/shard_map/ppermute | solution.py:319

commit v4 on v3

--- a/solution.py
+++ b/solution.py
@@ -144,8 +144,9 @@
     return turned
 
 
-def project_kernel(keep_ref, recv_ref, second_ref, out_ref):
+def project_kernel(keep_ref, recv_ref, second_ref, across_ref, keep_out_ref, send_out_ref):
     gy = lax.axis_index("gy")
+    x_half = lax.axis_index("gz") & 1
     rows = iota((R, R), 0)
     rank = ((rows >> 1) & 1) * 32 + (rows & 1) * 16 + (rows >> 2)
     picked = dot(onehot(rank == iota((R, R), 1)), second_ref[...])
@@ -154,7 +155,7 @@
     weights = jnp.concatenate([own, own], axis=1).astype(bf16)
     slot = iota((R, 128), 1) >> 5
 
-    def step(ip, carry):
+    def project(ip, store):
         sides = []
         for s in range(2):
             keep_high, keep_low = split(keep_ref[s, ip])
@@ -162,24 +163,44 @@
             sides.append(dot(weights, jnp.concatenate([keep_high, recv_high, keep_low, recv_low], axis=0)))
         for t in range(2):
             tiles = [sides[n // 2][:, n % 2 * 256 + t * 128 : n % 2 * 256 + (t + 1) * 128] for n in range(4)]
-            for d, tile in enumerate(turn_lanes(tiles, slot)):
-                out_ref[4 * t + d, ip] = tile
+            turned = turn_lanes(tiles, slot)
+            for d in range(0, 4, 2):
+                own = jnp.where(x_half == 0, turned[d], turned[d + 1])
+                other = jnp.where(x_half == 0, turned[d + 1], turned[d])
+                store(2 * t + d // 2, own, other)
+
+    def step(ip, carry):
+        def first(y, own, other):
+            across_ref[y, 0, ip] = own
+            across_ref[y, 1, ip] = other
+
+        def second(y, own, other):
+            keep_out_ref[y, ip] = own
+            send_out_ref[y, ip] = other
+
+        project(ip, first)
+        project(ip + HALF // 2, second)
         return carry
 
-    lax.fori_loop(0, HALF, step, 0, unroll=3)
+    lax.fori_loop(0, HALF // 2, step, 0)
 
 
 def local_projected(keep, recv, second):
+    part = (HALF // 2, R, 128)
     return pl.pallas_call(
         project_kernel,
-        out_shape=jax.ShapeDtypeStruct((GZ, HALF, R, 128), f32),
+        out_shape=[
+            jax.ShapeDtypeStruct((4, 2, *part), f32),
+            jax.ShapeDtypeStruct((4, *part), f32),
+            jax.ShapeDtypeStruct((4, *part), f32),
+        ],
         compiler_params=pltpu.CompilerParams(vmem_limit_bytes=16 * 2**20),
         cost_estimate=pl.CostEstimate(flops=10**9, bytes_accessed=8 * 2**20, transcendentals=0),
         name="projected",
     )(keep, recv, second)
 
 
-def gram_kernel(rows_ref, gram_ref, keep_ref, send_ref, columns_ref):
+def gram_kernel(rows_ref, keep_ref, send_ref, columns_ref):
     gy = lax.axis_index("gy")
     low_lanes = iota((GX * HALF, 128), 1) < 64
     for t in range(2):
@@ -194,20 +215,24 @@
                 top = g * CX + s * HALF
                 columns_ref[top : top + HALF, t * 128 : (t + 1) * 128] = sides[s][g * HALF : (g + 1) * HALF, :]
     parts = split3(columns_ref[...])
-    for n, (r, c) in enumerate(BLOCKS):
+    blocks = []
+    for r, c in BLOCKS:
         left = [part[r * 128 : (r + 1) * 128, :] for part in parts]
         right = [part[c * 128 : (c + 1) * 128, :] for part in parts]
-        gram_ref[n * 128 : (n + 1) * 128, :] = dot3(left, right, (1, 1))
+        blocks.append(dot3(left, right, (1, 1)))
+    for n in range(3):
+        keep_ref[0, n * 128 : (n + 1) * 128, :] = jnp.where(gy == 0, blocks[n], blocks[n + 3])
+        send_ref[0, n * 128 : (n + 1) * 128, :] = jnp.where(gy == 0, blocks[n + 3], blocks[n])
     low, high = columns_ref[:, :128], columns_ref[:, 128:]
-    keep_ref[...] = jnp.where(gy == 0, low, high)
-    send_ref[...] = jnp.where(gy == 0, high, low)
+    keep_ref[1] = jnp.where(gy == 0, low, high)
+    send_ref[1] = jnp.where(gy == 0, high, low)
 
 
 def local_gram(rows):
-    half = jax.ShapeDtypeStruct((NX, 128), f32)
+    half = jax.ShapeDtypeStruct((2, NX, 128), f32)
     return pl.pallas_call(
         gram_kernel,
-        out_shape=[jax.ShapeDtypeStruct((768, 128), f32), half, half],
+        out_shape=[half, half],
         scratch_shapes=[pltpu.VMEM((NX, 256), f32)],
         compiler_params=pltpu.CompilerParams(vmem_limit_bytes=8 * 2**20),
         name="gram",
@@ -252,11 +277,13 @@
     return jnp.concatenate(done, axis=0)[:, R:]
 
 
-def factor_kernel(gram_ref, start_ref, keep_ref, recv_ref, factor_ref, core_ref, high_ref, middle_ref, low_ref):
+def factor_kernel(own_ref, other_ref, start_ref, keep_ref, recv_ref, factor_ref, core_ref, high_ref, middle_ref, low_ref):
     gy = lax.axis_index("gy")
     parts_refs = (high_ref, middle_ref, low_ref)
     for n, (r, c) in enumerate(BLOCKS):
-        block = gram_ref[n * 128 : (n + 1) * 128, :]
+        rows = slice(n % 3 * 128, (n % 3 + 1) * 128)
+        own, other = own_ref[rows, :], other_ref[rows, :]
+        block = jnp.where(gy == n // 3, own, other)
         for ref, part in zip(parts_refs, split3(block)):
             ref[r * 128 : (r + 1) * 128, c * 128 : (c + 1) * 128] = part
         if r != c:
@@ -270,7 +297,7 @@
         inner = dot3(parts, parts, (1, 1))
         basis = dot3(split3(invert_lower(inner)), parts)
     factor_ref[...] = basis
-    keep, recv = keep_ref[...], recv_ref[...]
+    keep, recv = keep_ref[1], recv_ref[1]
     low, high = jnp.where(gy == 0, keep, recv), jnp.where(gy == 0, recv, keep)
     low_lanes = iota((NX, 128), 1) < 64
     columns = (
@@ -286,14 +313,14 @@
             core_ref[g, 4 * b : 4 * b + 4, :] = core[4 * g : 4 * g + 4, :]
 
 
-def factor_and_core(gram, start, keep, recv):
+def factor_and_core(own, other, start, keep, recv):
     return pl.pallas_call(
         factor_kernel,
         out_shape=[jax.ShapeDtypeStruct((R, NX), f32), jax.ShapeDtypeStruct((GX, 8, 128), f32)],
         scratch_shapes=[pltpu.VMEM((NX, NX), bf16)] * 3,
         compiler_params=pltpu.CompilerParams(vmem_limit_bytes=8 * 2**20),
         name="factor",
-    )(gram, start, keep, recv)
+    )(own, other, start, keep, recv)
 
 
 def order_kernel(core_ref, out_ref, turned_ref):
@@ -319,6 +346,15 @@
     return lax.ppermute(x, "gy", [(0, 1), (1, 0)])
 
 
+def swap_x(x):
+    return lax.ppermute(x, "gz", [(n, n ^ 1) for n in range(GZ)])
+
+
+def exchange_y(x):
+    groups = [[2 * y + x for y in range(4)] for x in range(2)]
+    return lax.all_to_all(x, "gz", 0, 0, tiled=True, axis_index_groups=groups)
+
+
 def exchange(x, axes):
     return lax.all_to_all(x, axes, 0, 0, tiled=True)
 
@@ -326,16 +362,22 @@
 def per_device(field, start_first, factor_second, factor_third, factor_vars):
     field = field.reshape(V, 2, HALF, CY, CZ)
     keep, send = local_depth(field, factor_third.T, factor_vars.T)
-    partial = local_projected(keep, swap(send), factor_second.T)
-    projected = jnp.sum(exchange(partial, "gz"), axis=0)
+    across, keep, send = local_projected(keep, swap(send), factor_second.T)
+    recv = swap_x(send)
+    across = jnp.sum(exchange_y(across), axis=0)
+    second = keep + recv
+    recv = swap_x(across[1])
+    second = jnp.sum(exchange_y(second), axis=0)
+    projected = jnp.concatenate([across[0] + recv, second], axis=0)
     projected = projected.reshape(HALF, GX, 4, 128).transpose(1, 0, 2, 3).reshape(GX, HALF * 4, 128)
     rows = exchange(projected, "gx").reshape(GX * HALF * 4, 128)
-    gram, keep, send = local_gram(rows)
+    keep, send = local_gram(rows)
     recv = swap(send)
-    gram = jnp.sum(exchange(gram.reshape(16, 48, 128), ("gy", "gz")), axis=0)
-    gram = jnp.sum(exchange(jnp.broadcast_to(gram, (16, 48, 128)), "gx"), axis=0)
-    gram = exchange(jnp.broadcast_to(gram, (16, 48, 128)), ("gy", "gz")).reshape(768, 128)
-    first_factor, core = factor_and_core(gram, start_first.T, keep, recv)
+    gram = (keep[0] + recv[0]).reshape(16, 24, 128)
+    gram = jnp.sum(exchange(gram, "gx"), axis=0)
+    gram = jnp.sum(exchange(jnp.broadcast_to(gram, (8, 24, 128)), "gz"), axis=0)
+    own = exchange(jnp.broadcast_to(gram, (16, 24, 128)), "gx").reshape(NX, 128)
+    first_factor, core = factor_and_core(own, swap(own), start_first.T, keep, recv)
     return first_factor.T, ordered(exchange(core, "gx"))
 
 

time: 149 us -> 142 us (0.953)
  blocking collectives: 111 us -> 72 us
  waiting for transfers between devices: 14.8 us -> 35.1 us
  starting transfers between devices: 4.21 us -> 13.5 us
  Pallas kernels: 16.7 us -> 18.3 us
    all_to_all x5, blocking collectives: 111 us -> 72 us  [exchange(): return lax.all_to_all(x, axes, 0, 0, tiled=True)]
    ppermute x0 -> x2, waiting for transfers between devices: none -> 23.8 us  [swap_x(): return lax.ppermute(x, 'gz', [(n, n ^ 1) for n in range(GZ)])]
    all_to_all x1 -> x2, waiting for transfers between devices: 9.14 us -> 3.67 us  [exchange_y(): return lax.all_to_all(x, 'gz', 0, 0, tiled=True, axis_index_groups=groups)]
    all_to_all x1 -> x2, starting transfers between devices: 3.71 us -> 9.01 us  [exchange_y(): return lax.all_to_all(x, 'gz', 0, 0, tiled=True, axis_index_groups=groups)]
    ppermute x0 -> x2, starting transfers between devices: none -> 4.26 us  [swap_x(): return lax.ppermute(x, 'gz', [(n, n ^ 1) for n in range(GZ)])]
    ppermute x2 -> x3, waiting for transfers between devices: 5.64 us -> 7.67 us  [swap(): return lax.ppermute(x, 'gy', [(0, 1), (1, 0)])]
    pallas_call x2, Pallas kernels: 3.06 us -> 4.55 us  [the longest x1 3.63 us: local_projected(): pl.pallas_call(project_kernel, out_shape=[jax.ShapeDtypeStruct((4, 2, *pa...]
  transfers between devices with their start and end apart: 3 -> 7, of which waited for: 3 -> 6; matrix products, arithmetic and copies ran while one was open for 0% -> 1% of each run, Pallas kernels for 0% -> 0%
where the time goes in v4:
time: 142 us; the launch traced here: 141 us
  blocking collectives  72 us (51%)
  waiting for transfers between devices  35.1 us (25%)
  Pallas kernels  18.3 us (13%)
  starting transfers between devices  13.5 us (10%)
    all_to_all x5, blocking collectives, exchange(): return lax.all_to_all(x, axes, 0, 0, tiled=True)  72 us
    ppermute x2, waiting for transfers between devices, swap_x(): return lax.ppermute(x, 'gz', [(n, n ^ 1) for n in range(GZ)])  23.8 us
    all_to_all x2, starting transfers between devices, exchange_y(): return lax.all_to_all(x, 'gz', 0, 0, tiled=True, axis_index_groups=groups)  9.01 us
    ppermute x3, waiting for transfers between devices, swap(): return lax.ppermute(x, 'gy', [(0, 1), (1, 0)])  7.67 us
    pallas_call x1, Pallas kernels, factor_and_core(): pl.pallas_call(factor_kernel, out_shape=[jax.ShapeDtypeStruct((R, NX), f3...  7.45 us
    pallas_call x1, Pallas kernels, local_depth(): pl.pallas_call(depth_kernel, in_specs=[far, far, far], out_specs=[near, n...  5.4 us
    ppermute x2, starting transfers between devices, swap_x(): return lax.ppermute(x, 'gz', [(n, n ^ 1) for n in range(GZ)])  4.26 us
    all_to_all x2, waiting for transfers between devices, exchange_y(): return lax.all_to_all(x, 'gz', 0, 0, tiled=True, axis_index_groups=groups)  3.67 us
  transfers between devices with their start and end apart: 7, of which 6 were waited for; matrix products, arithmetic and copies ran while one was open for 1% of the time, Pallas kernels for 0%

profile of v4, /device:TPU:2, one launch (start us, length us, event | category | flops | bytes accessed | tf_op | source)
XLA Modules:
  0.0 141.1 jit_solution(8073737724754914635)
XLA Ops:
  0.6 0.0 copy-start.1
  0.6 5.4 %depth.1 = (f32[2,12,48,512]{3,2,1,0:T(8,128)S(1)}, f32[2,12,48,512]{3,2,1,0:T(8,128)S(1)}) custom-call(bf16[32,2,12,48,128]{4,3,2,1,0:T(8,128)(2,1)} %bitcast.31, bf16[64,1024]{1,0:T(8,128)(2,1)} %bitcast.32, bf16[16,32]{1,0:T(8,128)(2,1)} %bitcast.34), custom_call_target="tpu_custom_call" | custom-call | flops 7000000000 | bytes 14680064 | tf_op jit(solution)/shard_map/depth/pallas_call | solution.py:106
  6.0 0.1 collective-permute-start
  6.1 4.5 %collective-permute-done.recv_ref = f32[2,12,48,512]{3,2,1,0:T(8,128)S(1)} collective-permute-done((f32[2,12,48,512]{3,2,1,0:T(8,128)S(1)}, f32[2,12,48,512]{3,2,1,0:T(8,128)S(1)}, u32[]{:S(2)}, u32[]{:S(2)}) %collective-permute-start) | collective-permute-done | bytes 2359328 | tf_op jit(solution)/shard_map/ppermute | solution.py:346
  10.7 0.0 copy-done.1
  10.7 3.6 %projected.1 = (f32[4,2,6,64,128]{4,3,2,1,0:T(8,128)}, f32[4,6,64,128]{3,2,1,0:T(8,128)S(1)}, f32[4,6,64,128]{3,2,1,0:T(8,128)S(1)}) custom-call(f32[2,12,48,512]{3,2,1,0:T(8,128)S(1)} %get-tuple-element.11.keep_ref, f32[2,12,48,512]{3,2,1,0:T(8,128)S(1)} %collective-permute-done.recv_ref, bf16[64,96]{1,0:T(8,128)(2,1)S(1)} %bitcast.26), custom_call_target="tpu_custom_call" | custom-call | flops 1000000000 | bytes 8388608 | tf_op jit(solution)/shard_map/projected/pallas_call | solution.py:190
  14.3 4.5 %all-to-all-start = ((f32[4,2,6,64,128]{4,3,2,1,0:T(8,128)}), f32[4,2,6,64,128]{4,3,2,1,0:T(8,128)S(1)}, u32[]{:S(2)}, u32[]{:S(2)}) async-start(f32[4,2,6,64,128]{4,3,2,1,0:T(8,128)} %get-tuple-element.13), calls=%async_computation | async-start | bytes 3145728 | tf_op jit(solution)/shard_map/all_to_all | solution.py:355
  18.8 2.1 %collective-permute-start.2 = (f32[4,6,64,128]{3,2,1,0:T(8,128)S(1)}, f32[4,6,64,128]{3,2,1,0:T(8,128)S(1)}, u32[]{:S(2)}, u32[]{:S(2)}) collective-permute-start(f32[4,6,64,128]{3,2,1,0:T(8,128)S(1)} %get-tuple-element.15), channel_id=1, source_target_pairs={{0,1},{1,0},{2,3},{3,2},{4,5},{5,4},{6,7},{7,6},{8,9},{9,8},{10,11... | collective-permute-start | bytes 2359304 | tf_op jit(solution)/shard_map/ppermute | solution.py:350
  20.9 18.7 %collective-permute-done.2 = f32[4,6,64,128]{3,2,1,0:T(8,128)S(1)} collective-permute-done((f32[4,6,64,128]{3,2,1,0:T(8,128)S(1)}, f32[4,6,64,128]{3,2,1,0:T(8,128)S(1)}, u32[]{:S(2)}, u32[]{:S(2)}) %collective-permute-start.2) | collective-permute-done | bytes 786464 | tf_op jit(solution)/shard_map/ppermute | solution.py:350
  39.6 1.0 add.14
  40.6 0.0 all-to-all-done
  40.6 4.5 %all-to-all-start.1 = ((f32[4,6,64,128]{3,2,1,0:T(8,128)}), f32[4,6,64,128]{3,2,1,0:T(8,128)S(1)}, u32[]{:S(2)}, u32[]{:S(2)}) async-start(f32[4,6,64,128]{3,2,1,0:T(8,128)} %add.14), calls=%async_computation.1 | async-start | bytes 1572864 | tf_op jit(solution)/shard_map/all_to_all | solution.py:355
  45.1 0.1 reduce_sum.36
  45.3 2.2 %collective-permute-start.1 = (f32[6,64,128]{2,1,0:T(8,128)S(1)}, f32[6,64,128]{2,1,0:T(8,128)S(1)}, u32[]{:S(2)}, u32[]{:S(2)}) collective-permute-start(f32[6,64,128]{2,1,0:T(8,128)S(1)} %slice_bitcast_fusion), channel_id=1, source_target_pairs={{0,1},{1,0},{2,3},{3,2},{4,5},{5,4},{6,7},{7,6},{8,9},{9,8},{10,11... | collective-permute-start | bytes 589832 | tf_op jit(solution)/shard_map/ppermute | solution.py:350
  47.4 5.1 %collective-permute-done.1 = f32[6,64,128]{2,1,0:T(8,128)S(1)} collective-permute-done((f32[6,64,128]{2,1,0:T(8,128)S(1)}, f32[6,64,128]{2,1,0:T(8,128)S(1)}, u32[]{:S(2)}, u32[]{:S(2)}) %collective-permute-start.1) | collective-permute-done | bytes 196640 | tf_op jit(solution)/shard_map/ppermute | solution.py:350
  52.6 3.7 %all-to-all-done.1 = f32[4,6,64,128]{3,2,1,0:T(8,128)S(1)} async-done(((f32[4,6,64,128]{3,2,1,0:T(8,128)}), f32[4,6,64,128]{3,2,1,0:T(8,128)S(1)}, u32[]{:S(2)}, u32[]{:S(2)}) %all-to-all-start.1) | async-done | bytes 786464 | tf_op jit(solution)/shard_map/all_to_all | solution.py:355
  56.3 0.0 copy-start
  56.4 0.1 copy.12
  56.5 20.5 %all_to_all.35 = f32[16,48,128]{2,1,0:T(8,128)S(1)} all-to-all(f32[16,48,128]{2,1,0:T(8,128)S(1)} %copy.12), channel_id=1, replica_groups=mesh['gx'=16,'gy'=2,'gz'=8] {'gx'}, dimensions={0} | all-to-all | bytes 786432 | tf_op jit(solution)/shard_map/all_to_all | solution.py:359
  77.0 0.9 gram.1
  77.9 0.1 collective-permute-start.3
  78.0 1.7 %collective-permute-done.3.recv_ref = f32[2,384,128]{2,1,0:T(8,128)S(1)} collective-permute-done((f32[2,384,128]{2,1,0:T(8,128)S(1)}, f32[2,384,128]{2,1,0:T(8,128)S(1)}, u32[]{:S(2)}, u32[]{:S(2)}) %collective-permute-start.3) | collective-permute-done | bytes 393248 | tf_op jit(solution)/shard_map/ppermute | solution.py:346
  79.8 13.8 %all_to_all.36 = f32[16,24,128]{2,1,0:T(8,128)S(1)} all-to-all(f32[16,24,128]{2,1,0:T(8,128)S(1)} %bitcast.29), channel_id=1, replica_groups=mesh['gx'=16,'gy'=2,'gz'=8] {'gx'}, dimensions={0} | all-to-all | bytes 393216 | tf_op jit(solution)/shard_map/all_to_all | solution.py:359
  93.6 12.2 %all_to_all.37 = f32[8,24,128]{2,1,0:T(8,128)S(1)} all-to-all(f32[8,24,128]{2,1,0:T(8,128)S(1)} %broadcast_in_dim.6), channel_id=1, replica_groups=mesh['gx'=16,'gy'=2,'gz'=8] {'gz'}, dimensions={0} | all-to-all | bytes 196608 | tf_op jit(solution)/shard_map/all_to_all | solution.py:359
  105.8 13.7 %all_to_all.38 = f32[16,24,128]{2,1,0:T(8,128)S(1)} all-to-all(f32[16,24,128]{2,1,0:T(8,128)S(1)} %broadcast_in_dim.7), channel_id=1, replica_groups=mesh['gx'=16,'gy'=2,'gz'=8] {'gx'}, dimensions={0} | all-to-all | bytes 393216 | tf_op jit(solution)/shard_map/all_to_all | solution.py:359
  119.5 0.0 collective-permute-start.4
  119.5 1.4 %collective-permute-done.4.other_ref = f32[384,128]{1,0:T(8,128)S(1)} collective-permute-done((f32[384,128]{1,0:T(8,128)S(1)}, f32[384,128]{1,0:T(8,128)S(1)}, u32[]{:S(2)}, u32[]{:S(2)}) %collective-permute-start.4) | collective-permute-done | bytes 196640 | tf_op jit(solution)/shard_map/ppermute | solution.py:346
  121.0 0.0 copy-done
  121.0 7.5 %factor.1 = (f32[64,384]{1,0:T(8,128)}, f32[16,8,128]{2,1,0:T(8,128)S(1)}) custom-call(f32[384,128]{1,0:T(8,128)S(1)} %bitcast.23, f32[384,128]{1,0:T(8,128)S(1)} %collective-permute-done.4.other_ref, f32[64,384]{1,0:T(8,128)S(1)} %bitcast.25, f32[2,384,128]{2,1,0:T(8,128)S(1)} %get-tuple-element.16.keep_ref, f32[2,384,128]{2,1,0:T(8,128)S(1)} %collective-permute-done.3.recv_ref), custom_call_target="tpu_custom_call" | custom-call | tf_op jit(solution)/shard_map/factor/pallas_call | solution.py:317
  128.4 11.8 %all_to_all.39 = f32[16,8,128]{2,1,0:T(8,128)S(1)} all-to-all(f32[16,8,128]{2,1,0:T(8,128)S(1)} %get-tuple-element.19), channel_id=1, replica_groups=mesh['gx'=16,'gy'=2,'gz'=8] {'gx'}, dimensions={0} | all-to-all | bytes 131072 | tf_op jit(solution)/shard_map/all_to_all | solution.py:359
  140.3 0.9 order.1
  (10 shorter events, 0.2 us)
Async XLA Ops:
  0.6 10.0 %copy-start.1 = (bf16[96,64]{0,1:T(8,128)(2,1)S(1)}, bf16[96,64]{0,1:T(8,128)(2,1)}, u32[]{:S(2)}) copy-start(bf16[96,64]{0,1:T(8,128)(2,1)} %param.7) | copy-start | bytes 36868
  6.0 4.6 %collective-permute-start = (f32[2,12,48,512]{3,2,1,0:T(8,128)S(1)}, f32[2,12,48,512]{3,2,1,0:T(8,128)S(1)}, u32[]{:S(2)}, u32[]{:S(2)}) collective-permute-start(f32[2,12,48,512]{3,2,1,0:T(8,128)S(1)} %get-tuple-element.12), channel_id=1, source_target_pairs={{0,8},{8,0},{1,9},{9,1},{2,10},{10,2},{3,11},{11,3},{4,12},{12,4},... | collective-permute-start | bytes 7077896 | tf_op jit(solution)/shard_map/ppermute | solution.py:346
  14.3 26.3 %all-to-all-start = ((f32[4,2,6,64,128]{4,3,2,1,0:T(8,128)}), f32[4,2,6,64,128]{4,3,2,1,0:T(8,128)S(1)}, u32[]{:S(2)}, u32[]{:S(2)}) async-start(f32[4,2,6,64,128]{4,3,2,1,0:T(8,128)} %get-tuple-element.13), calls=%async_computation | async-start | bytes 3145728 | tf_op jit(solution)/shard_map/all_to_all | solution.py:355
  18.8 20.8 %collective-permute-start.2 = (f32[4,6,64,128]{3,2,1,0:T(8,128)S(1)}, f32[4,6,64,128]{3,2,1,0:T(8,128)S(1)}, u32[]{:S(2)}, u32[]{:S(2)}) collective-permute-start(f32[4,6,64,128]{3,2,1,0:T(8,128)S(1)} %get-tuple-element.15), channel_id=1, source_target_pairs={{0,1},{1,0},{2,3},{3,2},{4,5},{5,4},{6,7},{7,6},{8,9},{9,8},{10,11... | collective-permute-start | bytes 2359304 | tf_op jit(solution)/shard_map/ppermute | solution.py:350
  40.6 15.6 %all-to-all-start.1 = ((f32[4,6,64,128]{3,2,1,0:T(8,128)}), f32[4,6,64,128]{3,2,1,0:T(8,128)S(1)}, u32[]{:S(2)}, u32[]{:S(2)}) async-start(f32[4,6,64,128]{3,2,1,0:T(8,128)} %add.14), calls=%async_computation.1 | async-start | bytes 1572864 | tf_op jit(solution)/shard_map/all_to_all | solution.py:355
  45.3 7.3 %collective-permute-start.1 = (f32[6,64,128]{2,1,0:T(8,128)S(1)}, f32[6,64,128]{2,1,0:T(8,128)S(1)}, u32[]{:S(2)}, u32[]{:S(2)}) collective-permute-start(f32[6,64,128]{2,1,0:T(8,128)S(1)} %slice_bitcast_fusion), channel_id=1, source_target_pairs={{0,1},{1,0},{2,3},{3,2},{4,5},{5,4},{6,7},{7,6},{8,9},{9,8},{10,11... | collective-permute-start | bytes 589832 | tf_op jit(solution)/shard_map/ppermute | solution.py:350
  56.3 64.7 %copy-start = (f32[384,64]{0,1:T(8,128)S(1)}, f32[384,64]{0,1:T(8,128)}, u32[]{:S(2)}) copy-start(f32[384,64]{0,1:T(8,128)} %param.6) | copy-start | bytes 294916
  77.9 1.8 %collective-permute-start.3 = (f32[2,384,128]{2,1,0:T(8,128)S(1)}, f32[2,384,128]{2,1,0:T(8,128)S(1)}, u32[]{:S(2)}, u32[]{:S(2)}) collective-permute-start(f32[2,384,128]{2,1,0:T(8,128)S(1)} %get-tuple-element.17), channel_id=1, source_target_pairs={{0,8},{8,0},{1,9},{9,1},{2,10},{10,2},{3,11},{11,3},{4,12},{12,4},... | collective-permute-start | bytes 1179656 | tf_op jit(solution)/shard_map/ppermute | solution.py:346
  119.5 1.4 %collective-permute-start.4 = (f32[384,128]{1,0:T(8,128)S(1)}, f32[384,128]{1,0:T(8,128)S(1)}, u32[]{:S(2)}, u32[]{:S(2)}) collective-permute-start(f32[384,128]{1,0:T(8,128)S(1)} %bitcast.22), channel_id=1, source_target_pairs={{0,8},{8,0},{1,9},{9,1},{2,10},{10,2},{3,11},{11,3},{4,12},{12,4},... | collective-permute-start | bytes 589832 | tf_op jit(solution)/shard_map/ppermute | solution.py:346

commit v5 on v4

--- a/solution.py
+++ b/solution.py
@@ -144,7 +144,7 @@
     return turned
 
 
-def project_kernel(keep_ref, recv_ref, second_ref, across_ref, keep_out_ref, send_out_ref):
+def project_kernel(keep_ref, recv_ref, second_ref, across_ref, keep_out_ref, send_out_ref, across_here, sems):
     gy = lax.axis_index("gy")
     x_half = lax.axis_index("gz") & 1
     rows = iota((R, R), 0)
@@ -169,24 +169,35 @@
                 other = jnp.where(x_half == 0, turned[d + 1], turned[d])
                 store(2 * t + d // 2, own, other)
 
-    def step(ip, carry):
-        def first(y, own, other):
-            across_ref[y, 0, ip] = own
-            across_ref[y, 1, ip] = other
-
-        def second(y, own, other):
+    def leave(ip):
+        return pltpu.make_async_copy(across_here.at[:, :, ip], across_ref.at[:, :, ip], sems.at[ip])
+
+    def first_half(ip, carry):
+        def store(y, own, other):
+            across_here[y, 0, ip] = own
+            across_here[y, 1, ip] = other
+
+        project(ip, store)
+        leave(ip).start()
+        return carry
+
+    def second_half(ip, carry):
+        def store(y, own, other):
             keep_out_ref[y, ip] = own
             send_out_ref[y, ip] = other
 
-        project(ip, first)
-        project(ip + HALF // 2, second)
+        project(ip + HALF // 2, store)
         return carry
 
-    lax.fori_loop(0, HALF // 2, step, 0)
+    lax.fori_loop(0, HALF // 2, first_half, 0, unroll=3)
+    lax.fori_loop(0, HALF // 2, second_half, 0, unroll=3)
+    for ip in range(HALF // 2):
+        leave(ip).wait()
 
 
 def local_projected(keep, recv, second):
     part = (HALF // 2, R, 128)
+    near = pl.BlockSpec(memory_space=pltpu.VMEM)
     return pl.pallas_call(
         project_kernel,
         out_shape=[
@@ -194,6 +205,8 @@
             jax.ShapeDtypeStruct((4, *part), f32),
             jax.ShapeDtypeStruct((4, *part), f32),
         ],
+        out_specs=[pl.BlockSpec(memory_space=pl.ANY), near, near],
+        scratch_shapes=[pltpu.VMEM((4, 2, *part), f32), pltpu.SemaphoreType.DMA((HALF // 2,))],
         compiler_params=pltpu.CompilerParams(vmem_limit_bytes=16 * 2**20),
         cost_estimate=pl.CostEstimate(flops=10**9, bytes_accessed=8 * 2**20, transcendentals=0),
         name="projected",

time: 142 us -> 141 us (level)
  no operation moved by 1% of the time
where the time goes in v5:
time: 141 us; the launch traced here: 140 us
  blocking collectives  72 us (51%)
  waiting for transfers between devices  35.1 us (25%)
  Pallas kernels  16.9 us (12%)
  starting transfers between devices  13.5 us (10%)
    all_to_all x5, blocking collectives, exchange(): return lax.all_to_all(x, axes, 0, 0, tiled=True)  72 us
    ppermute x2, waiting for transfers between devices, swap_x(): return lax.ppermute(x, 'gz', [(n, n ^ 1) for n in range(GZ)])  23.8 us
    all_to_all x2, starting transfers between devices, exchange_y(): return lax.all_to_all(x, 'gz', 0, 0, tiled=True, axis_index_groups=groups)  9.02 us
    ppermute x3, waiting for transfers between devices, swap(): return lax.ppermute(x, 'gy', [(0, 1), (1, 0)])  7.67 us
    pallas_call x1, Pallas kernels, factor_and_core(): pl.pallas_call(factor_kernel, out_shape=[jax.ShapeDtypeStruct((R, NX), f3...  7.45 us
    pallas_call x1, Pallas kernels, local_depth(): pl.pallas_call(depth_kernel, in_specs=[far, far, far], out_specs=[near, n...  5.4 us
    ppermute x2, starting transfers between devices, swap_x(): return lax.ppermute(x, 'gz', [(n, n ^ 1) for n in range(GZ)])  4.27 us
    all_to_all x2, waiting for transfers between devices, exchange_y(): return lax.all_to_all(x, 'gz', 0, 0, tiled=True, axis_index_groups=groups)  3.67 us
  transfers between devices with their start and end apart: 7, of which 6 were waited for; matrix products, arithmetic and copies ran while one was open for 1% of the time, Pallas kernels for 0%

profile of v5, /device:TPU:2, one launch (start us, length us, event | category | flops | bytes accessed | tf_op | source)
XLA Modules:
  0.0 139.7 jit_solution(5129515086997030065)
XLA Ops:
  0.6 0.0 copy-start.1
  0.6 5.4 %depth.1 = (f32[2,12,48,512]{3,2,1,0:T(8,128)S(1)}, f32[2,12,48,512]{3,2,1,0:T(8,128)S(1)}) custom-call(bf16[32,2,12,48,128]{4,3,2,1,0:T(8,128)(2,1)} %bitcast.31, bf16[64,1024]{1,0:T(8,128)(2,1)} %bitcast.32, bf16[16,32]{1,0:T(8,128)(2,1)} %bitcast.34), custom_call_target="tpu_custom_call" | custom-call | flops 7000000000 | bytes 14680064 | tf_op jit(solution)/shard_map/depth/pallas_call | solution.py:106
  6.0 0.1 collective-permute-start
  6.1 4.5 %collective-permute-done.recv_ref = f32[2,12,48,512]{3,2,1,0:T(8,128)S(1)} collective-permute-done((f32[2,12,48,512]{3,2,1,0:T(8,128)S(1)}, f32[2,12,48,512]{3,2,1,0:T(8,128)S(1)}, u32[]{:S(2)}, u32[]{:S(2)}) %collective-permute-start) | collective-permute-done | bytes 2359328 | tf_op jit(solution)/shard_map/ppermute | solution.py:359
  10.7 0.0 copy-done.1
  10.7 2.2 %projected.1 = (f32[4,2,6,64,128]{4,3,2,1,0:T(8,128)}, f32[4,6,64,128]{3,2,1,0:T(8,128)S(1)}, f32[4,6,64,128]{3,2,1,0:T(8,128)S(1)}) custom-call(f32[2,12,48,512]{3,2,1,0:T(8,128)S(1)} %get-tuple-element.11.keep_ref, f32[2,12,48,512]{3,2,1,0:T(8,128)S(1)} %collective-permute-done.recv_ref, bf16[64,96]{1,0:T(8,128)(2,1)S(1)} %bitcast.26), custom_call_target="tpu_custom_call" | custom-call | flops 1000000000 | bytes 8388608 | tf_op jit(solution)/shard_map/projected/pallas_call | solution.py:201
  12.9 4.5 %all-to-all-start = ((f32[4,2,6,64,128]{4,3,2,1,0:T(8,128)}), f32[4,2,6,64,128]{4,3,2,1,0:T(8,128)S(1)}, u32[]{:S(2)}, u32[]{:S(2)}) async-start(f32[4,2,6,64,128]{4,3,2,1,0:T(8,128)} %get-tuple-element.13), calls=%async_computation | async-start | bytes 3145728 | tf_op jit(solution)/shard_map/all_to_all | solution.py:368
  17.4 2.1 %collective-permute-start.2 = (f32[4,6,64,128]{3,2,1,0:T(8,128)S(1)}, f32[4,6,64,128]{3,2,1,0:T(8,128)S(1)}, u32[]{:S(2)}, u32[]{:S(2)}) collective-permute-start(f32[4,6,64,128]{3,2,1,0:T(8,128)S(1)} %get-tuple-element.15), channel_id=1, source_target_pairs={{0,1},{1,0},{2,3},{3,2},{4,5},{5,4},{6,7},{7,6},{8,9},{9,8},{10,11... | collective-permute-start | bytes 2359304 | tf_op jit(solution)/shard_map/ppermute | solution.py:363
  19.5 18.7 %collective-permute-done.2 = f32[4,6,64,128]{3,2,1,0:T(8,128)S(1)} collective-permute-done((f32[4,6,64,128]{3,2,1,0:T(8,128)S(1)}, f32[4,6,64,128]{3,2,1,0:T(8,128)S(1)}, u32[]{:S(2)}, u32[]{:S(2)}) %collective-permute-start.2) | collective-permute-done | bytes 786464 | tf_op jit(solution)/shard_map/ppermute | solution.py:363
  38.2 1.0 add.14
  39.2 0.0 all-to-all-done
  39.2 4.5 %all-to-all-start.1 = ((f32[4,6,64,128]{3,2,1,0:T(8,128)}), f32[4,6,64,128]{3,2,1,0:T(8,128)S(1)}, u32[]{:S(2)}, u32[]{:S(2)}) async-start(f32[4,6,64,128]{3,2,1,0:T(8,128)} %add.14), calls=%async_computation.1 | async-start | bytes 1572864 | tf_op jit(solution)/shard_map/all_to_all | solution.py:368
  43.7 0.1 reduce_sum.36
  43.9 2.2 %collective-permute-start.1 = (f32[6,64,128]{2,1,0:T(8,128)S(1)}, f32[6,64,128]{2,1,0:T(8,128)S(1)}, u32[]{:S(2)}, u32[]{:S(2)}) collective-permute-start(f32[6,64,128]{2,1,0:T(8,128)S(1)} %slice_bitcast_fusion), channel_id=1, source_target_pairs={{0,1},{1,0},{2,3},{3,2},{4,5},{5,4},{6,7},{7,6},{8,9},{9,8},{10,11... | collective-permute-start | bytes 589832 | tf_op jit(solution)/shard_map/ppermute | solution.py:363
  46.1 5.1 %collective-permute-done.1 = f32[6,64,128]{2,1,0:T(8,128)S(1)} collective-permute-done((f32[6,64,128]{2,1,0:T(8,128)S(1)}, f32[6,64,128]{2,1,0:T(8,128)S(1)}, u32[]{:S(2)}, u32[]{:S(2)}) %collective-permute-start.1) | collective-permute-done | bytes 196640 | tf_op jit(solution)/shard_map/ppermute | solution.py:363
  51.2 3.7 %all-to-all-done.1 = f32[4,6,64,128]{3,2,1,0:T(8,128)S(1)} async-done(((f32[4,6,64,128]{3,2,1,0:T(8,128)}), f32[4,6,64,128]{3,2,1,0:T(8,128)S(1)}, u32[]{:S(2)}, u32[]{:S(2)}) %all-to-all-start.1) | async-done | bytes 786464 | tf_op jit(solution)/shard_map/all_to_all | solution.py:368
  54.9 0.0 copy-start
  55.0 0.1 copy.12
  55.1 20.5 %all_to_all.35 = f32[16,48,128]{2,1,0:T(8,128)S(1)} all-to-all(f32[16,48,128]{2,1,0:T(8,128)S(1)} %copy.12), channel_id=1, replica_groups=mesh['gx'=16,'gy'=2,'gz'=8] {'gx'}, dimensions={0} | all-to-all | bytes 786432 | tf_op jit(solution)/shard_map/all_to_all | solution.py:372
  75.6 0.9 gram.1
  76.5 0.1 collective-permute-start.3
  76.6 1.7 %collective-permute-done.3.recv_ref = f32[2,384,128]{2,1,0:T(8,128)S(1)} collective-permute-done((f32[2,384,128]{2,1,0:T(8,128)S(1)}, f32[2,384,128]{2,1,0:T(8,128)S(1)}, u32[]{:S(2)}, u32[]{:S(2)}) %collective-permute-start.3) | collective-permute-done | bytes 393248 | tf_op jit(solution)/shard_map/ppermute | solution.py:359
  78.4 13.8 %all_to_all.36 = f32[16,24,128]{2,1,0:T(8,128)S(1)} all-to-all(f32[16,24,128]{2,1,0:T(8,128)S(1)} %bitcast.29), channel_id=1, replica_groups=mesh['gx'=16,'gy'=2,'gz'=8] {'gx'}, dimensions={0} | all-to-all | bytes 393216 | tf_op jit(solution)/shard_map/all_to_all | solution.py:372
  92.2 12.2 %all_to_all.37 = f32[8,24,128]{2,1,0:T(8,128)S(1)} all-to-all(f32[8,24,128]{2,1,0:T(8,128)S(1)} %broadcast_in_dim.6), channel_id=1, replica_groups=mesh['gx'=16,'gy'=2,'gz'=8] {'gz'}, dimensions={0} | all-to-all | bytes 196608 | tf_op jit(solution)/shard_map/all_to_all | solution.py:372
  104.4 13.7 %all_to_all.38 = f32[16,24,128]{2,1,0:T(8,128)S(1)} all-to-all(f32[16,24,128]{2,1,0:T(8,128)S(1)} %broadcast_in_dim.7), channel_id=1, replica_groups=mesh['gx'=16,'gy'=2,'gz'=8] {'gx'}, dimensions={0} | all-to-all | bytes 393216 | tf_op jit(solution)/shard_map/all_to_all | solution.py:372
  118.1 0.0 collective-permute-start.4
  118.2 1.4 %collective-permute-done.4.other_ref = f32[384,128]{1,0:T(8,128)S(1)} collective-permute-done((f32[384,128]{1,0:T(8,128)S(1)}, f32[384,128]{1,0:T(8,128)S(1)}, u32[]{:S(2)}, u32[]{:S(2)}) %collective-permute-start.4) | collective-permute-done | bytes 196640 | tf_op jit(solution)/shard_map/ppermute | solution.py:359
  119.6 0.0 copy-done
  119.6 7.5 %factor.1 = (f32[64,384]{1,0:T(8,128)}, f32[16,8,128]{2,1,0:T(8,128)S(1)}) custom-call(f32[384,128]{1,0:T(8,128)S(1)} %bitcast.23, f32[384,128]{1,0:T(8,128)S(1)} %collective-permute-done.4.other_ref, f32[64,384]{1,0:T(8,128)S(1)} %bitcast.25, f32[2,384,128]{2,1,0:T(8,128)S(1)} %get-tuple-element.16.keep_ref, f32[2,384,128]{2,1,0:T(8,128)S(1)} %collective-permute-done.3.recv_ref), custom_call_target="tpu_custom_call" | custom-call | tf_op jit(solution)/shard_map/factor/pallas_call | solution.py:330
  127.0 11.8 %all_to_all.39 = f32[16,8,128]{2,1,0:T(8,128)S(1)} all-to-all(f32[16,8,128]{2,1,0:T(8,128)S(1)} %get-tuple-element.19), channel_id=1, replica_groups=mesh['gx'=16,'gy'=2,'gz'=8] {'gx'}, dimensions={0} | all-to-all | bytes 131072 | tf_op jit(solution)/shard_map/all_to_all | solution.py:372
  138.9 0.9 order.1
  (10 shorter events, 0.2 us)
Async XLA Ops:
  0.6 10.0 %copy-start.1 = (bf16[96,64]{0,1:T(8,128)(2,1)S(1)}, bf16[96,64]{0,1:T(8,128)(2,1)}, u32[]{:S(2)}) copy-start(bf16[96,64]{0,1:T(8,128)(2,1)} %param.7) | copy-start | bytes 36868
  6.0 4.6 %collective-permute-start = (f32[2,12,48,512]{3,2,1,0:T(8,128)S(1)}, f32[2,12,48,512]{3,2,1,0:T(8,128)S(1)}, u32[]{:S(2)}, u32[]{:S(2)}) collective-permute-start(f32[2,12,48,512]{3,2,1,0:T(8,128)S(1)} %get-tuple-element.12), channel_id=1, source_target_pairs={{0,8},{8,0},{1,9},{9,1},{2,10},{10,2},{3,11},{11,3},{4,12},{12,4},... | collective-permute-start | bytes 7077896 | tf_op jit(solution)/shard_map/ppermute | solution.py:359
  12.9 26.3 %all-to-all-start = ((f32[4,2,6,64,128]{4,3,2,1,0:T(8,128)}), f32[4,2,6,64,128]{4,3,2,1,0:T(8,128)S(1)}, u32[]{:S(2)}, u32[]{:S(2)}) async-start(f32[4,2,6,64,128]{4,3,2,1,0:T(8,128)} %get-tuple-element.13), calls=%async_computation | async-start | bytes 3145728 | tf_op jit(solution)/shard_map/all_to_all | solution.py:368
  17.4 20.8 %collective-permute-start.2 = (f32[4,6,64,128]{3,2,1,0:T(8,128)S(1)}, f32[4,6,64,128]{3,2,1,0:T(8,128)S(1)}, u32[]{:S(2)}, u32[]{:S(2)}) collective-permute-start(f32[4,6,64,128]{3,2,1,0:T(8,128)S(1)} %get-tuple-element.15), channel_id=1, source_target_pairs={{0,1},{1,0},{2,3},{3,2},{4,5},{5,4},{6,7},{7,6},{8,9},{9,8},{10,11... | collective-permute-start | bytes 2359304 | tf_op jit(solution)/shard_map/ppermute | solution.py:363
  39.2 15.6 %all-to-all-start.1 = ((f32[4,6,64,128]{3,2,1,0:T(8,128)}), f32[4,6,64,128]{3,2,1,0:T(8,128)S(1)}, u32[]{:S(2)}, u32[]{:S(2)}) async-start(f32[4,6,64,128]{3,2,1,0:T(8,128)} %add.14), calls=%async_computation.1 | async-start | bytes 1572864 | tf_op jit(solution)/shard_map/all_to_all | solution.py:368
  43.9 7.3 %collective-permute-start.1 = (f32[6,64,128]{2,1,0:T(8,128)S(1)}, f32[6,64,128]{2,1,0:T(8,128)S(1)}, u32[]{:S(2)}, u32[]{:S(2)}) collective-permute-start(f32[6,64,128]{2,1,0:T(8,128)S(1)} %slice_bitcast_fusion), channel_id=1, source_target_pairs={{0,1},{1,0},{2,3},{3,2},{4,5},{5,4},{6,7},{7,6},{8,9},{9,8},{10,11... | collective-permute-start | bytes 589832 | tf_op jit(solution)/shard_map/ppermute | solution.py:363
  54.9 64.7 %copy-start = (f32[384,64]{0,1:T(8,128)S(1)}, f32[384,64]{0,1:T(8,128)}, u32[]{:S(2)}) copy-start(f32[384,64]{0,1:T(8,128)} %param.6) | copy-start | bytes 294916
  76.5 1.8 %collective-permute-start.3 = (f32[2,384,128]{2,1,0:T(8,128)S(1)}, f32[2,384,128]{2,1,0:T(8,128)S(1)}, u32[]{:S(2)}, u32[]{:S(2)}) collective-permute-start(f32[2,384,128]{2,1,0:T(8,128)S(1)} %get-tuple-element.17), channel_id=1, source_target_pairs={{0,8},{8,0},{1,9},{9,1},{2,10},{10,2},{3,11},{11,3},{4,12},{12,4},... | collective-permute-start | bytes 1179656 | tf_op jit(solution)/shard_map/ppermute | solution.py:359
  118.1 1.4 %collective-permute-start.4 = (f32[384,128]{1,0:T(8,128)S(1)}, f32[384,128]{1,0:T(8,128)S(1)}, u32[]{:S(2)}, u32[]{:S(2)}) collective-permute-start(f32[384,128]{1,0:T(8,128)S(1)} %bitcast.22), channel_id=1, source_target_pairs={{0,8},{8,0},{1,9},{9,1},{2,10},{10,2},{3,11},{11,3},{4,12},{12,4},... | collective-permute-start | bytes 589832 | tf_op jit(solution)/shard_map/ppermute | solution.py:359

commit v6 on v5

--- a/solution.py
+++ b/solution.py
@@ -1,3 +1,5 @@
+import functools
+
 import jax
 import jax.numpy as jnp
 from jax import lax
@@ -17,7 +19,8 @@
 HALF = CX // 2
 EH = RV // 2
 NX = 384
-IPB = 4
+IPB = 3
+EARLY = 9
 STEP = 16
 BLOCKS = ((0, 0), (0, 1), (0, 2), (1, 1), (1, 2), (2, 2))
 
@@ -41,21 +44,21 @@
 
 
 def depth_kernel(
-    field_ref, third_ref, vars_ref, keep_ref, send_ref, cells_ref, third_here, vars_here, mix_ref, cols_ref, left_ref, sems
+    first, count, field_ref, third_ref, vars_ref, keep_ref, send_ref, cells_ref, third_here, vars_here, mix_ref, cols_ref, left_ref, sems
 ):
     gy = lax.axis_index("gy")
     gz = lax.axis_index("gz")
 
     def fetch(chunk):
-        cells = pl.ds(chunk * IPB, IPB)
-        return pltpu.make_async_copy(field_ref.at[:, :, cells], cells_ref.at[:, :, cells], sems.at[chunk])
+        source = field_ref.at[:, :, pl.ds(first + chunk * IPB, IPB)]
+        return pltpu.make_async_copy(source, cells_ref.at[:, :, pl.ds(chunk * IPB, IPB)], sems.at[chunk])
 
     third_part = third_ref.at[:, pl.ds(pl.multiple_of(gz * CZ, CZ), CZ)]
-    third_copy = pltpu.make_async_copy(third_part, third_here, sems.at[HALF // IPB])
-    vars_copy = pltpu.make_async_copy(vars_ref, vars_here, sems.at[HALF // IPB + 1])
+    third_copy = pltpu.make_async_copy(third_part, third_here, sems.at[count // IPB])
+    vars_copy = pltpu.make_async_copy(vars_ref, vars_here, sems.at[count // IPB + 1])
     third_copy.start()
     vars_copy.start()
-    for chunk in range(HALF // IPB):
+    for chunk in range(count // IPB):
         fetch(chunk).start()
 
     rows = iota((128, RV), 0)
@@ -96,29 +99,29 @@
             half[:, pl.ds(chunk * IPB, IPB), :, n % 2 * 256 : (n % 2 + 1) * 256] = depth[n]
         return carry
 
-    lax.fori_loop(0, HALF // IPB, step, 0)
-
-
-def local_depth(field, third, weights):
-    half = jax.ShapeDtypeStruct((2, HALF, CY, 512), f32)
+    lax.fori_loop(0, count // IPB, step, 0)
+
+
+def local_depth(field, third, weights, first, count):
+    half = jax.ShapeDtypeStruct((2, count, CY, 512), f32)
     far = pl.BlockSpec(memory_space=pltpu.HBM)
     near = pl.BlockSpec(memory_space=pltpu.VMEM)
     return pl.pallas_call(
-        depth_kernel,
+        functools.partial(depth_kernel, first, count),
         in_specs=[far, far, far],
         out_specs=[near, near],
         out_shape=[half, half],
         scratch_shapes=[
-            pltpu.VMEM((V, 2, HALF, CY, CZ), bf16),
+            pltpu.VMEM((V, 2, count, CY, CZ), bf16),
             pltpu.VMEM((R, CZ), bf16),
             pltpu.VMEM((RV, V), bf16),
             pltpu.VMEM((128, 256), bf16),
             pltpu.VMEM((512, 256), bf16),
             pltpu.VMEM((2, 8 * IPB * CY, 512), bf16),
-            pltpu.SemaphoreType.DMA((HALF // IPB + 2,)),
+            pltpu.SemaphoreType.DMA((count // IPB + 2,)),
         ],
         compiler_params=pltpu.CompilerParams(vmem_limit_bytes=28 * 2**20),
-        cost_estimate=pl.CostEstimate(flops=7 * 10**9, bytes_accessed=14 * 2**20, transcendentals=0),
+        cost_estimate=pl.CostEstimate(flops=count * 6 * 10**8, bytes_accessed=count * 2**20, transcendentals=0),
         name="depth",
     )(*(pltpu.with_memory_space_constraint(x, pltpu.HBM) for x in (field, third, weights)))
 
@@ -144,7 +147,7 @@
     return turned
 
 
-def project_kernel(keep_ref, recv_ref, second_ref, across_ref, keep_out_ref, send_out_ref, across_here, sems):
+def project_kernel(keep_ref, recv_ref, keep_late_ref, recv_late_ref, second_ref, across_ref, keep_out_ref, send_out_ref, across_here, sems):
     gy = lax.axis_index("gy")
     x_half = lax.axis_index("gz") & 1
     rows = iota((R, R), 0)
@@ -155,7 +158,7 @@
     weights = jnp.concatenate([own, own], axis=1).astype(bf16)
     slot = iota((R, 128), 1) >> 5
 
-    def project(ip, store):
+    def project(ip, store, keep_ref=keep_ref, recv_ref=recv_ref):
         sides = []
         for s in range(2):
             keep_high, keep_low = split(keep_ref[s, ip])
@@ -189,13 +192,22 @@
         project(ip + HALF // 2, store)
         return carry
 
+    def last_cells(ip, carry):
+        def store(y, own, other):
+            keep_out_ref[y, ip] = own
+            send_out_ref[y, ip] = other
+
+        project(ip + HALF // 2 - EARLY, store, keep_late_ref, recv_late_ref)
+        return carry
+
     lax.fori_loop(0, HALF // 2, first_half, 0, unroll=3)
-    lax.fori_loop(0, HALF // 2, second_half, 0, unroll=3)
+    lax.fori_loop(0, EARLY - HALF // 2, second_half, 0, unroll=3)
+    lax.fori_loop(EARLY - HALF // 2, HALF // 2, last_cells, 0, unroll=3)
     for ip in range(HALF // 2):
         leave(ip).wait()
 
 
-def local_projected(keep, recv, second):
+def local_projected(keep, recv, keep_late, recv_late, second):
     part = (HALF // 2, R, 128)
     near = pl.BlockSpec(memory_space=pltpu.VMEM)
     return pl.pallas_call(
@@ -210,7 +222,7 @@
         compiler_params=pltpu.CompilerParams(vmem_limit_bytes=16 * 2**20),
         cost_estimate=pl.CostEstimate(flops=10**9, bytes_accessed=8 * 2**20, transcendentals=0),
         name="projected",
-    )(keep, recv, second)
+    )(keep, recv, keep_late, recv_late, second)
 
 
 def gram_kernel(rows_ref, keep_ref, send_ref, columns_ref):
@@ -374,8 +386,10 @@
 
 def per_device(field, start_first, factor_second, factor_third, factor_vars):
     field = field.reshape(V, 2, HALF, CY, CZ)
-    keep, send = local_depth(field, factor_third.T, factor_vars.T)
-    across, keep, send = local_projected(keep, swap(send), factor_second.T)
+    third, weights = factor_third.T, factor_vars.T
+    keep, send = local_depth(field, third, weights, 0, EARLY)
+    keep_late, send_late = local_depth(field, third, weights, EARLY, HALF - EARLY)
+    across, keep, send = local_projected(keep, swap(send), keep_late, swap(send_late), factor_second.T)
     recv = swap_x(send)
     across = jnp.sum(exchange_y(across), axis=0)
     second = keep + recv

time: 141 us -> 141 us (level)
  waiting for transfers between devices: 35.1 us -> 32.7 us
  Pallas kernels: 16.9 us -> 18.4 us
    all_to_all x2, waiting for transfers between devices: 3.67 us -> 9 us  [exchange_y(): return lax.all_to_all(x, 'gz', 0, 0, tiled=True, axis_index_groups=groups)]
    ppermute x2, waiting for transfers between devices: 23.8 us -> 18.9 us  [swap_x(): return lax.ppermute(x, 'gz', [(n, n ^ 1) for n in range(GZ)])]
    ppermute x3 -> x4, waiting for transfers between devices: 7.67 us -> 4.78 us  [swap(): return lax.ppermute(x, 'gy', [(0, 1), (1, 0)])]
    pallas_call x1 -> x2, Pallas kernels: 5.4 us -> 7.02 us  [local_depth(): pl.pallas_call(functools.partial(depth_kernel, first, count), in_specs=[f...]
  transfers between devices with their start and end apart: 7 -> 8, of which waited for: 6 -> 5; matrix products, arithmetic and copies ran while one was open for 1% -> 1% of each run, Pallas kernels for 0% -> 2%
where the time goes in v6:
time: 141 us; the launch traced here: 140 us
  blocking collectives  72.3 us (51%)
  waiting for transfers between devices  32.7 us (23%)
  Pallas kernels  18.4 us (13%)
  starting transfers between devices  14.1 us (10%)
    all_to_all x5, blocking collectives, exchange(): return lax.all_to_all(x, axes, 0, 0, tiled=True)  72.3 us
    ppermute x2, waiting for transfers between devices, swap_x(): return lax.ppermute(x, 'gz', [(n, n ^ 1) for n in range(GZ)])  18.9 us
    all_to_all x2, waiting for transfers between devices, exchange_y(): return lax.all_to_all(x, 'gz', 0, 0, tiled=True, axis_index_groups=groups)  9 us
    all_to_all x2, starting transfers between devices, exchange_y(): return lax.all_to_all(x, 'gz', 0, 0, tiled=True, axis_index_groups=groups)  9 us
    pallas_call x1, Pallas kernels, factor_and_core(): pl.pallas_call(factor_kernel, out_shape=[jax.ShapeDtypeStruct((R, NX), f3...  7.45 us
    pallas_call x2, Pallas kernels, local_depth(): pl.pallas_call(functools.partial(depth_kernel, first, count), in_specs=[f...  7.02 us
    ppermute x4, waiting for transfers between devices, swap(): return lax.ppermute(x, 'gy', [(0, 1), (1, 0)])  4.78 us
    ppermute x2, starting transfers between devices, swap_x(): return lax.ppermute(x, 'gz', [(n, n ^ 1) for n in range(GZ)])  4.34 us
  transfers between devices with their start and end apart: 8, of which 5 were waited for; matrix products, arithmetic and copies ran while one was open for 1% of the time, Pallas kernels for 2%

profile of v6, /device:TPU:2, one launch (start us, length us, event | category | flops | bytes accessed | tf_op | source)
XLA Modules:
  0.0 139.8 jit_solution(11060633493179358773)
XLA Ops:
  0.6 4.4 %depth.2 = (f32[2,9,48,512]{3,2,1,0:T(8,128)S(1)}, f32[2,9,48,512]{3,2,1,0:T(8,128)S(1)}) custom-call(bf16[32,2,12,48,128]{4,3,2,1,0:T(8,128)(2,1)} %bitcast.27, bf16[64,1024]{1,0:T(8,128)(2,1)} %bitcast.33, bf16[16,32]{1,0:T(8,128)(2,1)} %bitcast.35), custom_call_target="tpu_custom_call" | custom-call | flops 5400000000 | bytes 9437184 | tf_op jit(solution)/shard_map/depth/pallas_call | solution.py:109
  5.0 0.0 copy-start.1
  5.0 0.1 collective-permute-start
  5.1 2.6 %depth.3 = (f32[2,3,48,512]{3,2,1,0:T(8,128)S(1)}, f32[2,3,48,512]{3,2,1,0:T(8,128)S(1)}) custom-call(bf16[32,2,12,48,128]{4,3,2,1,0:T(8,128)(2,1)} %bitcast.28, bf16[64,1024]{1,0:T(8,128)(2,1)} %bitcast.34, bf16[16,32]{1,0:T(8,128)(2,1)} %bitcast.36), custom_call_target="tpu_custom_call" | custom-call | flops 1800000000 | bytes 3145728 | tf_op jit(solution)/shard_map/depth/pallas_call | solution.py:109
  7.8 0.6 collective-permute-start.1
  8.4 1.6 %collective-permute-done.1.recv_late_ref = f32[2,3,48,512]{3,2,1,0:T(8,128)S(1)} collective-permute-done((f32[2,3,48,512]{3,2,1,0:T(8,128)S(1)}, f32[2,3,48,512]{3,2,1,0:T(8,128)S(1)}, u32[]{:S(2)}, u32[]{:S(2)}) %collective-permute-start.1) | collective-permute-done | bytes 589856 | tf_op jit(solution)/shard_map/ppermute | solution.py:371
  10.0 0.0 collective-permute-done.recv_ref
  10.0 0.0 copy-done.1
  10.0 2.2 %projected.1 = (f32[4,2,6,64,128]{4,3,2,1,0:T(8,128)}, f32[4,6,64,128]{3,2,1,0:T(8,128)S(1)}, f32[4,6,64,128]{3,2,1,0:T(8,128)S(1)}) custom-call(f32[2,9,48,512]{3,2,1,0:T(8,128)S(1)} %get-tuple-element.13.keep_ref, f32[2,9,48,512]{3,2,1,0:T(8,128)S(1)} %collective-permute-done.recv_ref, f32[2,3,48,512]{3,2,1,0:T(8,128)S(1)} %get-tuple-element.15.keep_late_ref, ...), custom_call_target="tpu_custom_call" | custom-call | flops 1000000000 | bytes 8388608 | tf_op jit(solution)/shard_map/projected/pallas_call | solution.py:213
  12.2 4.5 %all-to-all-start = ((f32[4,2,6,64,128]{4,3,2,1,0:T(8,128)}), f32[4,2,6,64,128]{4,3,2,1,0:T(8,128)S(1)}, u32[]{:S(2)}, u32[]{:S(2)}) async-start(f32[4,2,6,64,128]{4,3,2,1,0:T(8,128)} %get-tuple-element.17), calls=%async_computation | async-start | bytes 3145728 | tf_op jit(solution)/shard_map/all_to_all | solution.py:380
  16.6 2.1 %collective-permute-start.3 = (f32[4,6,64,128]{3,2,1,0:T(8,128)S(1)}, f32[4,6,64,128]{3,2,1,0:T(8,128)S(1)}, u32[]{:S(2)}, u32[]{:S(2)}) collective-permute-start(f32[4,6,64,128]{3,2,1,0:T(8,128)S(1)} %get-tuple-element.19), channel_id=1, source_target_pairs={{0,1},{1,0},{2,3},{3,2},{4,5},{5,4},{6,7},{7,6},{8,9},{9,8},{10,11... | collective-permute-start | bytes 2359304 | tf_op jit(solution)/shard_map/ppermute | solution.py:375
  18.8 18.9 %collective-permute-done.3 = f32[4,6,64,128]{3,2,1,0:T(8,128)S(1)} collective-permute-done((f32[4,6,64,128]{3,2,1,0:T(8,128)S(1)}, f32[4,6,64,128]{3,2,1,0:T(8,128)S(1)}, u32[]{:S(2)}, u32[]{:S(2)}) %collective-permute-start.3) | collective-permute-done | bytes 786464 | tf_op jit(solution)/shard_map/ppermute | solution.py:375
  37.7 1.0 add.14
  38.7 0.0 all-to-all-done
  38.7 4.5 %all-to-all-start.1 = ((f32[4,6,64,128]{3,2,1,0:T(8,128)}), f32[4,6,64,128]{3,2,1,0:T(8,128)S(1)}, u32[]{:S(2)}, u32[]{:S(2)}) async-start(f32[4,6,64,128]{3,2,1,0:T(8,128)} %add.14), calls=%async_computation.1 | async-start | bytes 1572864 | tf_op jit(solution)/shard_map/all_to_all | solution.py:380
  43.2 0.1 reduce_sum.36
  43.3 2.2 %collective-permute-start.2 = (f32[6,64,128]{2,1,0:T(8,128)S(1)}, f32[6,64,128]{2,1,0:T(8,128)S(1)}, u32[]{:S(2)}, u32[]{:S(2)}) collective-permute-start(f32[6,64,128]{2,1,0:T(8,128)S(1)} %slice_bitcast_fusion), channel_id=1, source_target_pairs={{0,1},{1,0},{2,3},{3,2},{4,5},{5,4},{6,7},{7,6},{8,9},{9,8},{10,11... | collective-permute-start | bytes 589832 | tf_op jit(solution)/shard_map/ppermute | solution.py:375
  45.5 9.0 %all-to-all-done.1 = f32[4,6,64,128]{3,2,1,0:T(8,128)S(1)} async-done(((f32[4,6,64,128]{3,2,1,0:T(8,128)}), f32[4,6,64,128]{3,2,1,0:T(8,128)S(1)}, u32[]{:S(2)}, u32[]{:S(2)}) %all-to-all-start.1) | async-done | bytes 786464 | tf_op jit(solution)/shard_map/all_to_all | solution.py:380
  54.6 0.0 collective-permute-done.2
  54.7 0.1 copy.12
  54.9 0.0 copy-start
  54.9 20.8 %all_to_all.35 = f32[16,48,128]{2,1,0:T(8,128)S(1)} all-to-all(f32[16,48,128]{2,1,0:T(8,128)S(1)} %copy.12), channel_id=1, replica_groups=mesh['gx'=16,'gy'=2,'gz'=8] {'gx'}, dimensions={0} | all-to-all | bytes 786432 | tf_op jit(solution)/shard_map/all_to_all | solution.py:384
  75.7 0.9 gram.1
  76.6 0.1 collective-permute-start.4
  76.7 1.7 %collective-permute-done.4.recv_ref = f32[2,384,128]{2,1,0:T(8,128)S(1)} collective-permute-done((f32[2,384,128]{2,1,0:T(8,128)S(1)}, f32[2,384,128]{2,1,0:T(8,128)S(1)}, u32[]{:S(2)}, u32[]{:S(2)}) %collective-permute-start.4) | collective-permute-done | bytes 393248 | tf_op jit(solution)/shard_map/ppermute | solution.py:371
  78.4 14.0 %all_to_all.36 = f32[16,24,128]{2,1,0:T(8,128)S(1)} all-to-all(f32[16,24,128]{2,1,0:T(8,128)S(1)} %bitcast.31), channel_id=1, replica_groups=mesh['gx'=16,'gy'=2,'gz'=8] {'gx'}, dimensions={0} | all-to-all | bytes 393216 | tf_op jit(solution)/shard_map/all_to_all | solution.py:384
  92.4 12.0 %all_to_all.37 = f32[8,24,128]{2,1,0:T(8,128)S(1)} all-to-all(f32[8,24,128]{2,1,0:T(8,128)S(1)} %broadcast_in_dim.6), channel_id=1, replica_groups=mesh['gx'=16,'gy'=2,'gz'=8] {'gz'}, dimensions={0} | all-to-all | bytes 196608 | tf_op jit(solution)/shard_map/all_to_all | solution.py:384
  104.4 13.7 %all_to_all.38 = f32[16,24,128]{2,1,0:T(8,128)S(1)} all-to-all(f32[16,24,128]{2,1,0:T(8,128)S(1)} %broadcast_in_dim.7), channel_id=1, replica_groups=mesh['gx'=16,'gy'=2,'gz'=8] {'gx'}, dimensions={0} | all-to-all | bytes 393216 | tf_op jit(solution)/shard_map/all_to_all | solution.py:384
  118.2 0.0 collective-permute-start.5
  118.2 1.4 %collective-permute-done.5.other_ref = f32[384,128]{1,0:T(8,128)S(1)} collective-permute-done((f32[384,128]{1,0:T(8,128)S(1)}, f32[384,128]{1,0:T(8,128)S(1)}, u32[]{:S(2)}, u32[]{:S(2)}) %collective-permute-start.5) | collective-permute-done | bytes 196640 | tf_op jit(solution)/shard_map/ppermute | solution.py:371
  119.6 0.0 copy-done
  119.6 7.5 %factor.1 = (f32[64,384]{1,0:T(8,128)}, f32[16,8,128]{2,1,0:T(8,128)S(1)}) custom-call(f32[384,128]{1,0:T(8,128)S(1)} %bitcast.23, f32[384,128]{1,0:T(8,128)S(1)} %collective-permute-done.5.other_ref, f32[64,384]{1,0:T(8,128)S(1)} %bitcast.25, f32[2,384,128]{2,1,0:T(8,128)S(1)} %get-tuple-element.20.keep_ref, f32[2,384,128]{2,1,0:T(8,128)S(1)} %collective-permute-done.4.recv_ref), custom_call_target="tpu_custom_call" | custom-call | tf_op jit(solution)/shard_map/factor/pallas_call | solution.py:342
  127.1 11.8 %all_to_all.39 = f32[16,8,128]{2,1,0:T(8,128)S(1)} all-to-all(f32[16,8,128]{2,1,0:T(8,128)S(1)} %get-tuple-element.23), channel_id=1, replica_groups=mesh['gx'=16,'gy'=2,'gz'=8] {'gx'}, dimensions={0} | all-to-all | bytes 131072 | tf_op jit(solution)/shard_map/all_to_all | solution.py:384
  138.9 0.9 order.1
  (10 shorter events, 0.2 us)
Async XLA Ops:
  5.0 5.0 %copy-start.1 = (bf16[96,64]{0,1:T(8,128)(2,1)S(1)}, bf16[96,64]{0,1:T(8,128)(2,1)}, u32[]{:S(2)}) copy-start(bf16[96,64]{0,1:T(8,128)(2,1)} %param.7) | copy-start | bytes 36868
  5.0 4.9 %collective-permute-start = (f32[2,9,48,512]{3,2,1,0:T(8,128)S(1)}, f32[2,9,48,512]{3,2,1,0:T(8,128)S(1)}, u32[]{:S(2)}, u32[]{:S(2)}) collective-permute-start(f32[2,9,48,512]{3,2,1,0:T(8,128)S(1)} %get-tuple-element.14), channel_id=1, source_target_pairs={{0,8},{8,0},{1,9},{9,1},{2,10},{10,2},{3,11},{11,3},{4,12},{12,4},... | collective-permute-start | bytes 5308424 | tf_op jit(solution)/shard_map/ppermute | solution.py:371
  7.8 2.2 %collective-permute-start.1 = (f32[2,3,48,512]{3,2,1,0:T(8,128)S(1)}, f32[2,3,48,512]{3,2,1,0:T(8,128)S(1)}, u32[]{:S(2)}, u32[]{:S(2)}) collective-permute-start(f32[2,3,48,512]{3,2,1,0:T(8,128)S(1)} %get-tuple-element.16), channel_id=1, source_target_pairs={{0,8},{8,0},{1,9},{9,1},{2,10},{10,2},{3,11},{11,3},{4,12},{12,4},... | collective-permute-start | bytes 1769480 | tf_op jit(solution)/shard_map/ppermute | solution.py:371
  12.2 26.5 %all-to-all-start = ((f32[4,2,6,64,128]{4,3,2,1,0:T(8,128)}), f32[4,2,6,64,128]{4,3,2,1,0:T(8,128)S(1)}, u32[]{:S(2)}, u32[]{:S(2)}) async-start(f32[4,2,6,64,128]{4,3,2,1,0:T(8,128)} %get-tuple-element.17), calls=%async_computation | async-start | bytes 3145728 | tf_op jit(solution)/shard_map/all_to_all | solution.py:380
  16.6 21.0 %collective-permute-start.3 = (f32[4,6,64,128]{3,2,1,0:T(8,128)S(1)}, f32[4,6,64,128]{3,2,1,0:T(8,128)S(1)}, u32[]{:S(2)}, u32[]{:S(2)}) collective-permute-start(f32[4,6,64,128]{3,2,1,0:T(8,128)S(1)} %get-tuple-element.19), channel_id=1, source_target_pairs={{0,1},{1,0},{2,3},{3,2},{4,5},{5,4},{6,7},{7,6},{8,9},{9,8},{10,11... | collective-permute-start | bytes 2359304 | tf_op jit(solution)/shard_map/ppermute | solution.py:375
  38.7 15.9 %all-to-all-start.1 = ((f32[4,6,64,128]{3,2,1,0:T(8,128)}), f32[4,6,64,128]{3,2,1,0:T(8,128)S(1)}, u32[]{:S(2)}, u32[]{:S(2)}) async-start(f32[4,6,64,128]{3,2,1,0:T(8,128)} %add.14), calls=%async_computation.1 | async-start | bytes 1572864 | tf_op jit(solution)/shard_map/all_to_all | solution.py:380
  43.3 11.3 %collective-permute-start.2 = (f32[6,64,128]{2,1,0:T(8,128)S(1)}, f32[6,64,128]{2,1,0:T(8,128)S(1)}, u32[]{:S(2)}, u32[]{:S(2)}) collective-permute-start(f32[6,64,128]{2,1,0:T(8,128)S(1)} %slice_bitcast_fusion), channel_id=1, source_target_pairs={{0,1},{1,0},{2,3},{3,2},{4,5},{5,4},{6,7},{7,6},{8,9},{9,8},{10,11... | collective-permute-start | bytes 589832 | tf_op jit(solution)/shard_map/ppermute | solution.py:375
  54.9 64.8 %copy-start = (f32[384,64]{0,1:T(8,128)S(1)}, f32[384,64]{0,1:T(8,128)}, u32[]{:S(2)}) copy-start(f32[384,64]{0,1:T(8,128)} %param.6) | copy-start | bytes 294916
  76.6 1.8 %collective-permute-start.4 = (f32[2,384,128]{2,1,0:T(8,128)S(1)}, f32[2,384,128]{2,1,0:T(8,128)S(1)}, u32[]{:S(2)}, u32[]{:S(2)}) collective-permute-start(f32[2,384,128]{2,1,0:T(8,128)S(1)} %get-tuple-element.21), channel_id=1, source_target_pairs={{0,8},{8,0},{1,9},{9,1},{2,10},{10,2},{3,11},{11,3},{4,12},{12,4},... | collective-permute-start | bytes 1179656 | tf_op jit(solution)/shard_map/ppermute | solution.py:371
  118.2 1.4 %collective-permute-start.5 = (f32[384,128]{1,0:T(8,128)S(1)}, f32[384,128]{1,0:T(8,128)S(1)}, u32[]{:S(2)}, u32[]{:S(2)}) collective-permute-start(f32[384,128]{1,0:T(8,128)S(1)} %bitcast.22), channel_id=1, source_target_pairs={{0,8},{8,0},{1,9},{9,1},{2,10},{10,2},{3,11},{11,3},{4,12},{12,4},... | collective-permute-start | bytes 589832 | tf_op jit(solution)/shard_map/ppermute | solution.py:371
